TPU v7x, 32 devices: a whole 2x2x4 slice. The times are simulated.
32 devices in a mesh: rep: 4 (over x, core), shard: 8 (over z, y).
Axes of the slice: x: 2, y: 2, z: 4, core: 2. Of those that a mesh axis runs over, the one named last changes fastest.
Arguments:
- tokens: bfloat16 [256, 128, 768], P(('rep', 'shard')), may hold values from -6 to 6
- word_counts: int32 [256], P(('rep', 'shard')), may hold values from 1 to 28
- region_counts: int32 [256], P(('rep', 'shard')), may hold values from 10 to 100
- qkv_weight: float32 [2304, 768], P('shard'), may hold values from -0.21875 to 0.21875
- qkv_bias: float32 [1536], P('shard'), may hold values from -3 to 3
- out_weight: float32 [768, 768], P('shard'), may hold values from -0.875 to 0.875
- out_bias: float32 [768], P('shard'), may hold values from -3 to 3
- attn_gain: float32 [768], P('shard'), may hold values from 0.5 to 1.5
- attn_shift: float32 [768], P('shard'), may hold values from -2 to 2
- up_weight: float32 [3072, 768], P('shard'), may hold values from -0.21875 to 0.21875
- up_bias: float32 [3072], P('shard'), may hold values from -3 to 3
- down_weight: float32 [768, 3072], P('shard'), may hold values from -0.109375 to 0.109375
- down_bias: float32 [768], P('shard'), may hold values from -2 to 2
- ffn_gain: float32 [768], P('shard'), may hold values from 0.5 to 1.5
- ffn_shift: float32 [768], P('shard'), may hold values from -2 to 2
- cotangent: bfloat16 [256, 128, 768], P(('rep', 'shard')), may hold values from -6 to 6
Outputs:
- layer_out: bfloat16 [256, 128, 768], P(('rep', 'shard'))
- tokens_grad: float32 [256, 128, 768], P(('rep', 'shard'))
- qkv_weight_grad: float32 [2304, 768], P('shard')
- qkv_bias_grad: float32 [1536], P('shard')
- out_weight_grad: float32 [768, 768], P('shard')
- out_bias_grad: float32 [768], P('shard')
- attn_gain_grad: float32 [768], P('shard')
- attn_shift_grad: float32 [768], P('shard')
- up_weight_grad: float32 [3072, 768], P('shard')
- up_bias_grad: float32 [3072], P('shard')
- down_weight_grad: float32 [768, 3072], P('shard')
- down_bias_grad: float32 [768], P('shard')
- ffn_gain_grad: float32 [768], P('shard')
- ffn_shift_grad: float32 [768], P('shard')
All inputs are finite; a program needn't handle non-finite values.
Results may differ from a plain program's by a relative error of at most 0.015.
The roundings to bfloat16 on the way count: a program that leaves them out, or rounds other values in their place, can miss the bound.
Values may be sent and summed in bfloat16 or wider, within the bound.
No kernel may reach another device: no remote copies, remote signals or barrier semaphores. Data moves between devices by JAX's collectives and lax.ppermute only.
A program may use at most 256 MiB of HBM per device.

v0:
```python
import functools

import jax
import jax.numpy as jnp
import numpy as np
from jax import lax
from jax.experimental import pallas as pl
from jax.experimental.pallas import tpu as pltpu
from jax.sharding import PartitionSpec as P

HEADS = 12
WORDS_MAX = 28
EPS = 1e-05
BF = jnp.bfloat16
F32 = jnp.float32
ANY = pl.BlockSpec(memory_space=pl.ANY)
SMEM = pl.BlockSpec(memory_space=pltpu.SMEM)
HBM, VMEM = pltpu.HBM, pltpu.VMEM
TOKEN = jax.ShapeDtypeStruct((8, 128), F32)
WHOLE = pl.BlockSpec(memory_space=pltpu.VMEM)
SQRT_HALF = 0.7071067811865476
INV_SQRT_2PI = 0.3989422804014327


def nt(a, b):
    return lax.dot_general(a, b, (((1,), (1,)), ((), ())), preferred_element_type=F32)


def nn(a, b):
    return jnp.dot(a, b, preferred_element_type=F32)


def tn(a, b):
    return lax.dot_general(a, b, (((0,), (0,)), ((), ())), preferred_element_type=F32)


def fixed(shape):
    return pl.BlockSpec(shape, lambda i: (0,) * len(shape))


def rows(shape):
    return pl.BlockSpec(shape, lambda i: (i,) + (0,) * (len(shape) - 1))


def far(value):
    return pltpu.with_memory_space_constraint(value, HBM)


def near(value):
    return pltpu.with_memory_space_constraint(value, VMEM)


def kernel_call(body, deps, in_specs, args, mebibytes=8, **options):
    count, extra = len(args), len(deps)

    def inner(*refs):
        body(*refs[:count], *refs[count + extra :])

    call = pl.pallas_call(
        inner, in_specs=list(in_specs) + [ANY] * extra, compiler_params=params(mebibytes), **options
    )
    return call(*args, *deps)


def params(mebibytes):
    return pltpu.CompilerParams(vmem_limit_bytes=mebibytes * 1024 * 1024)


def piece_place(meta, cc, a, b, rz, local_rows, start, height, width):
    x0, z0, y0 = meta[0], meta[2], meta[3]
    y_rel = jnp.where(cc == 0, a, b)
    x_rel = jnp.where(cc == 0, b, a)
    shard = (z0 ^ rz) * 2 + (y0 ^ y_rel)
    row = shard * local_rows + cc * height + start
    col = (x0 ^ x_rel) * width
    return pl.multiple_of(row, 16), pl.multiple_of(col, 128)


def piece_copies(meta, pieces, whole, sems, local_rows, first, height, width):
    copies = []
    for number, ref in enumerate(pieces):
        cc = meta[1] if number < 2 else 1 - meta[1]
        a = number % 2
        for b in range(2):
            for rz in range(4):
                row, col = piece_place(meta, cc, a, b, rz, local_rows, 0, height, width)
                copies.append(
                    pltpu.make_async_copy(
                        ref.at[b * 4 + rz, pl.ds(first, height), :],
                        whole.at[pl.ds(row, height), pl.ds(col, width)],
                        sems.at[len(copies)],
                    )
                )
    return copies


def tile_waits(whole, outs, sems, count, first, height, span):
    return [
        pltpu.make_async_copy(
            whole.at[pl.ds(0, height), pl.ds(0, span)],
            ref.at[0, pl.ds(first, height), pl.ds(0, span)],
            sems.at[number * count + i],
        )
        for number, ref in enumerate(outs[1:])
        for i in range(count)
    ]


def load_copies(fast, meta, refs, whole, sems, first):
    if not fast:
        return [pltpu.make_async_copy(refs[0], whole, sems.at[0])]
    local_rows, cols = whole.shape[0] // 8, whole.shape[1]
    if len(refs) == 1:
        height, width = local_rows // 2, cols // 2
        return [
            pltpu.make_async_copy(
                refs[0].at[(x * 2 + c) * 8 + shard],
                whole.at[
                    pl.ds(shard * local_rows + c * height, height), pl.ds(x * width, width)
                ],
                sems.at[(x * 2 + c) * 8 + shard],
            )
            for x in range(2)
            for c in range(2)
            for shard in range(8)
        ]
    return piece_copies(meta, refs, whole, sems, local_rows, first, local_rows // 2, cols // 2)


def go(copies):
    for copy in copies:
        copy.start()


def done(copies):
    for copy in copies:
        copy.wait()


def key_mask(words, regions, shape, axis):
    place = lax.broadcasted_iota(jnp.int32, shape, axis)
    return (place < words) | ((place >= WORDS_MAX) & (place < WORDS_MAX + regions))


def split_heads(block):
    low = lax.broadcasted_iota(jnp.int32, block.shape, 1) < 64
    zero = jnp.zeros_like(block)
    return jnp.concatenate([jnp.where(low, block, zero), jnp.where(low, zero, block)], axis=0)


def turn_heads(block):
    n = block.shape[0]
    return jnp.concatenate([block[:, :n].T, block[:, n:].T], axis=1)


def norm_parts(value):
    center = value - jnp.mean(value, axis=-1, keepdims=True)
    rstd = lax.rsqrt(jnp.mean(center * center, axis=-1, keepdims=True) + EPS)
    return center * rstd, rstd


def norm_back(grad, xhat, rstd, gain):
    scaled = grad * gain
    mean_one = jnp.mean(scaled, axis=-1, keepdims=True)
    mean_two = jnp.mean(scaled * xhat, axis=-1, keepdims=True)
    return rstd * (scaled - mean_one - xhat * mean_two)


def attention_kernel(fast, n_in, *refs):
    meta, words, regions = refs[:3]
    x_ref, vec_ref = refs[3:5]
    pieces = refs[5 : 5 + n_in]
    (joined_ref, probs_ref, mix_ref, low_ref, xhat_ref, rstd_ref, wqkv_out, wo_out) = refs[
        5 + n_in : 13 + n_in
    ]
    wqkv, wo, sem_a, sem_b, sem_c = refs[13 + n_in :]
    step = pl.program_id(0)
    d = x_ref.shape[1]
    seq = probs_ref.shape[2]

    @pl.when(step == 0)
    def _():
        if fast:
            first = load_copies(fast, meta, pieces, wqkv, sem_a, 0)
            second = load_copies(fast, meta, pieces, wo, sem_b, wqkv.shape[0] // 16)
        else:
            first = load_copies(fast, meta, pieces[:1], wqkv, sem_a, 0)
            second = load_copies(fast, meta, pieces[1:], wo, sem_b, 0)
        go(first)
        go(second)
        done(first)
        done(second)

    saves = [
        pltpu.make_async_copy(wqkv, wqkv_out, sem_c.at[0]),
        pltpu.make_async_copy(wo, wo_out, sem_c.at[1]),
    ]

    @pl.when(step == 0)
    def _():
        go(saves)

    x = x_ref[...]
    bq = vec_ref[:, :d]
    bv = vec_ref[:, d : 2 * d]
    joined_ref[:, :d] = (nt(x, wqkv[:d, :]) + bq).astype(BF) * BF(0.125)
    joined_ref[:, d : 2 * d] = nt(x, wqkv[d : 2 * d, :]).astype(BF)
    joined_ref[:, 2 * d :] = (nt(x, wqkv[2 * d :, :]) + bv).astype(BF)
    per_step = x_ref.shape[0] // seq
    for p in range(per_step):
        pair = step * per_step + p
        valid = key_mask(words[pair], regions[pair], (seq, 2 * seq), 0)
        here = pl.ds(p * seq, seq)
        for h in range(d // 128):
            cols = pl.ds(h * 128, 128)
            queries = split_heads(joined_ref[here, pl.ds(h * 128, 128)])
            keys = joined_ref[here, pl.ds(d + h * 128, 128)]
            values = split_heads(joined_ref[here, pl.ds(2 * d + h * 128, 128)])
            scores = jnp.where(valid, nt(keys, queries), -1000000000.0)
            exponent = jnp.exp(scores - jnp.max(scores, axis=0, keepdims=True))
            probs = exponent * (1.0 / jnp.sum(exponent, axis=0, keepdims=True))
            probs = probs.astype(BF)
            probs_ref[p, h] = probs
            mix_ref[here, cols] = nn(turn_heads(probs), values).astype(BF)
    first_sum = x.astype(F32) + nt(mix_ref[...], wo[...]) + vec_ref[:, 2 * d : 3 * d]
    xhat, rstd = norm_parts(first_sum)
    xhat_ref[...] = xhat
    rstd_ref[...] = jnp.broadcast_to(rstd, rstd_ref.shape)
    low_ref[...] = (xhat * vec_ref[:, 3 * d : 4 * d] + vec_ref[:, 4 * d : 5 * d]).astype(BF)

    @pl.when(step == pl.num_programs(0) - 1)
    def _():
        done(saves)


def attention_forward(fast, meta, words, regions, x, vec, pieces, seq, deps=()):
    n, d = x.shape
    tile = 2 * seq
    shapes = [
        HBM((n, 3 * d), BF),
        HBM((n // seq, d // 128, seq, 2 * seq), BF),
        HBM((n, d), BF),
        HBM((n, d), BF),
        HBM((n, d), F32),
        HBM((n, 128), F32),
        HBM((3 * d, d), BF),
        HBM((d, d), BF),
    ]
    return kernel_call(
        functools.partial(attention_kernel, fast, len(pieces)),
        deps,
        [SMEM] * 3 + [rows((tile, d)), fixed(vec.shape)] + [ANY] * len(pieces),
        [meta, words, regions, far(x), vec, *map(far, pieces)],
        grid=(n // tile,),
        out_specs=[
            rows((tile, 3 * d)),
            rows((2, d // 128, seq, 2 * seq)),
            rows((tile, d)),
            rows((tile, d)),
            rows((tile, d)),
            rows((tile, 128)),
            ANY,
            ANY,
        ],
        out_shape=shapes,
        scratch_shapes=[
            pltpu.VMEM((3 * d, d), BF),
            pltpu.VMEM((d, d), BF),
            pltpu.SemaphoreType.DMA((32,)),
            pltpu.SemaphoreType.DMA((32,)),
            pltpu.SemaphoreType.DMA((2,)),
        ],
        cost_estimate=pl.CostEstimate(
            flops=2 * n * d * 4 * d, bytes_accessed=16 * n * d, transcendentals=0
        ),
        mebibytes=17,
        name="attention_forward",
    )


def up_kernel(fast, n_in, *refs):
    meta, low_far, bias_ref = refs[:3]
    pieces = refs[3 : 3 + n_in]
    act_ref, slope_ref, token_ref, low_ref, w, sem_a, sem_b = refs[3 + n_in :]
    token_ref[...] = jnp.zeros_like(token_ref)
    n = low_ref.shape[0]
    tile, width = 256, w.shape[0] // 4
    reads = [pltpu.make_async_copy(low_far, low_ref, sem_b.at[0])]
    go(reads)
    loads = load_copies(fast, meta, pieces, w, sem_a, 0)
    parts = [loads] + [[]] * 3
    if len(loads) == 32:
        parts = [[v for k, v in enumerate(loads) if k % 8 // 2 == j] for j in range(4)]
    for part in parts:
        go(part)
    done(reads)
    for j in range(4):
        done(parts[j])
        here = slice(j * width, (j + 1) * width)
        for i in range(n // tile):
            part = slice(i * tile, (i + 1) * tile)
            hidden = nt(low_ref[part, :], w[here, :]) + bias_ref[:, here]
            phi = 0.5 + 0.5 * lax.erf(hidden * SQRT_HALF)
            act_ref[part, here] = (hidden * phi).astype(BF)
            bell = jnp.exp(hidden * hidden * -0.5) * INV_SQRT_2PI
            slope_ref[part, here] = (phi + hidden * bell).astype(BF)


def up_forward(fast, meta, low, bias, pieces, deps=()):
    n, d = low.shape
    ff = bias.shape[1]
    return kernel_call(
        functools.partial(up_kernel, fast, len(pieces)),
        deps,
        [SMEM, ANY, WHOLE] + [ANY] * len(pieces),
        [meta, far(low), bias, *map(far, pieces)],
        out_specs=[WHOLE] * 3,
        out_shape=[VMEM((n, ff), BF), VMEM((n, ff), BF), TOKEN],
        scratch_shapes=[
            pltpu.VMEM((n, d), BF),
            pltpu.VMEM((ff, d), BF),
            pltpu.SemaphoreType.DMA((32,)),
            pltpu.SemaphoreType.DMA((1,)),
        ],
        cost_estimate=pl.CostEstimate(
            flops=4 * n * d * ff, bytes_accessed=4 * n * ff, transcendentals=0
        ),
        mebibytes=14,
        name="up_forward",
    )


def down_kernel(fast, n_in, seq, *refs):
    meta, words, regions = refs[:3]
    act_ref, slope_ref, xhat_far, vec_ref, cot_far = refs[3:8]
    pieces = refs[8 : 8 + n_in]
    outs_end = 14 + n_in + (2 if fast else 1)
    out_far, second_far, feed_ref, sums_ref, w, _ = refs[8 + n_in : 14 + n_in]
    grads = refs[14 + n_in : outs_end]
    xhat_ref, cot_ref, out_ref, second_ref, whole = refs[outs_end:-3]
    sem_a, sem_b, sem_c = refs[-3:]
    n, d = feed_ref.shape
    ff = act_ref.shape[1]
    tile = 256
    count = n // tile
    loads = load_copies(fast, meta, pieces, w, sem_a, 0)
    go(loads)
    reads, writes = [], []
    for i in range(count):
        part = pl.ds(i * tile, tile)
        reads.append(
            [
                pltpu.make_async_copy(xhat_far.at[part], xhat_ref.at[part], sem_b.at[0, i]),
                pltpu.make_async_copy(cot_far.at[part], cot_ref.at[part], sem_b.at[1, i]),
            ]
        )
        writes += [
            pltpu.make_async_copy(out_ref.at[part], out_far.at[part], sem_b.at[2, i]),
            pltpu.make_async_copy(second_ref.at[part], second_far.at[part], sem_b.at[3, i]),
        ]
    for pair in reads:
        go(pair)
    gain_one, shift_one = vec_ref[:, :d], vec_ref[:, d : 2 * d]
    bias, gain, shift = vec_ref[:, 2 * d : 3 * d], vec_ref[:, 3 * d : 4 * d], vec_ref[:, 4 * d :]
    done(loads)
    sums = [jnp.zeros((1, d), F32)] * 3
    product = nt(act_ref[:tile, :], w[...])
    for i in range(count):
        part = slice(i * tile, (i + 1) * tile)
        done(reads[i])
        if i:
            go(writes[2 * i - 2 : 2 * i])
        this = product
        if i + 1 < count:
            product = nt(act_ref[(i + 1) * tile : (i + 2) * tile, :], w[...])
        second_sum = xhat_ref[part, :] * gain_one + shift_one + this + bias
        xhat, rstd = norm_parts(second_sum)
        first = i * (tile // seq)
        keep = jnp.concatenate(
            [
                key_mask(words[first + p], regions[first + p], (seq, 128), 0)
                for p in range(tile // seq)
            ],
            axis=0,
        )[:, :1]
        out_ref[part, :] = jnp.where(keep, xhat * gain + shift, 0.0).astype(BF)
        grad = jnp.where(keep, cot_ref[part, :].astype(F32), 0.0)
        second = norm_back(grad, xhat, rstd, gain)
        second_ref[part, :] = second
        feed = second.astype(BF)
        feed_ref[part, :] = feed
        for k, value in enumerate((grad * xhat, grad, feed.astype(F32))):
            sums[k] = sums[k] + jnp.sum(value, axis=0, keepdims=True)
    go(writes[-2:])
    for k in range(3):
        sums_ref[k : k + 1, :] = sums[k]
    waits = []
    width, span = ff // 4, ff // 8
    for i in range(4):
        here = slice(i * width, (i + 1) * width)
        whole[:, here] = tn(feed_ref[...], act_ref[:, here]).astype(BF)
        if fast:
            for k in range(2):
                chunk = (i % 2) * 2 + k
                copies = tile_copies(
                    meta, whole, grads, sem_c.at[2 * i + k], range(8), [i // 2], d // 8,
                    chunk * (d // 16), d // 16, ff // 2, (chunk * span, span),
                )
                go(copies)
                waits += tile_waits(
                    whole, grads, sem_c.at[2 * i + k], 8, chunk * (d // 16), d // 16, span
                )
    if not fast:
        waits = [pltpu.make_async_copy(whole, grads[0], sem_c.at[0, 0])]
        go(waits)
    done(waits)
    done(writes)


def down_forward(
    fast, meta, words, regions, act, slope, xhat, vec, cot, pieces, seq, deps=()
):
    n, ff = act.shape
    d = xhat.shape[1]
    shapes = grad_shapes(fast, d, ff)
    return kernel_call(
        functools.partial(down_kernel, fast, len(pieces), seq),
        deps,
        [SMEM] * 3 + [WHOLE, WHOLE, ANY, WHOLE, ANY] + [ANY] * len(pieces),
        [meta, words, regions, near(act), near(slope), far(xhat), vec, far(cot), *map(far, pieces[:-1]), *pieces[-1:]],
        out_specs=[ANY, ANY, WHOLE, WHOLE, WHOLE, WHOLE] + [WHOLE, ANY][-len(shapes) :],
        out_shape=[
            HBM((n, d), BF),
            HBM((n, d), F32),
            VMEM((n, d), BF),
            jax.ShapeDtypeStruct((8, d), F32),
            VMEM((d, ff), BF),
            VMEM((n, ff), BF),
        ]
        + shapes,
        scratch_shapes=[
            pltpu.VMEM((n, d), F32),
            pltpu.VMEM((n, d), BF),
            pltpu.VMEM((n, d), BF),
            pltpu.VMEM((n, d), F32),
            pltpu.VMEM((d, ff), BF),
            pltpu.SemaphoreType.DMA((32,)),
            pltpu.SemaphoreType.DMA((4, n // 256)),
            pltpu.SemaphoreType.DMA((8, 16)),
        ],
        cost_estimate=pl.CostEstimate(
            flops=12 * n * d * ff, bytes_accessed=2 * n * ff, transcendentals=0
        ),
        input_output_aliases={4: 5},
        mebibytes=24,
        name="down_forward",
    )


def hidden_grad_kernel(feed_ref, slope_ref, w, hidden_ref, bias_ref):
    width = 512
    for i in range(slope_ref.shape[1] // width):
        here = slice(i * width, (i + 1) * width)
        hidden = nn(feed_ref[...], w[:, here]) * slope_ref[:, here].astype(F32)
        hidden = hidden.astype(BF)
        hidden_ref[:, here] = hidden
        bias_ref[:, here] = jnp.sum(hidden.astype(F32), axis=0, keepdims=True)


def hidden_grad(feed, slope, w, deps=()):
    n, ff = slope.shape
    d = feed.shape[1]
    return kernel_call(
        hidden_grad_kernel,
        deps,
        [WHOLE] * 3,
        [near(feed), near(slope), near(w)],
        out_specs=[WHOLE] * 2,
        out_shape=[VMEM((n, ff), BF), jax.ShapeDtypeStruct((1, ff), F32)],
        cost_estimate=pl.CostEstimate(
            flops=4 * n * d * ff, bytes_accessed=4 * n * ff, transcendentals=0
        ),
        mebibytes=10,
        name="hidden_grad",
    )


def grad_shapes(fast, total_rows, cols):
    if fast:
        width = min(total_rows, cols) // 2
        shape = (16, total_rows * cols // (32 * width), width)
        return [VMEM(shape, BF), HBM(shape, BF)]
    return [HBM((total_rows, cols), BF)]


def tile_copies(meta, whole, outs, sems, shards, sides, local_rows, first, height, width, cols=None):
    x0, c0, z0, y0 = meta[0], meta[1], meta[2], meta[3]
    offset, span = (0, width) if cols is None else cols
    there = pl.ds(0, span)
    copies = []
    for number, ref in enumerate(outs):
        cc = c0 ^ number
        for shard in shards:
            for side in sides:
                y_rel, x_rel = y0 ^ (shard % 2), x0 ^ side
                a = jnp.where(cc == 0, y_rel, x_rel)
                b = jnp.where(cc == 0, x_rel, y_rel)
                row = pl.multiple_of(shard * local_rows + cc * height, 16)
                col = pl.multiple_of(side * width + offset, 128)
                place = a * 8 + b * 4 + (z0 ^ (shard // 2))
                if number == 0:
                    static = pl.ds(side * width + offset, span)
                    ref[place, pl.ds(first, height), there] = whole[pl.ds(row, height), static]
                    continue
                copies.append(
                    pltpu.make_async_copy(
                        whole.at[pl.ds(row, height), pl.ds(col, span)],
                        ref.at[place, pl.ds(first, height), there],
                        sems.at[len(copies)],
                    )
                )
    return copies


def up_grad_kernel(fast, *refs):
    meta, hidden_ref, low_far, wu_far, *others_far = refs[:8]
    outs = refs[8 : (10 if fast else 9)]
    token_ref, _, wu_ref, *others = refs[10 if fast else 9 : -5]
    low_ref, whole, sems, sem_b, sem_c = refs[-5:]
    reads = [pltpu.make_async_copy(low_far, low_ref, sem_b.at[0])]
    go(reads)
    ahead = load_copies(fast, meta, [wu_far], wu_ref, sem_c, 0)
    for i, (source, target) in enumerate(zip(others_far, others)):
        ahead.append(pltpu.make_async_copy(source, target, sem_b.at[1 + i]))
    go(ahead)
    token_ref[...] = jnp.zeros_like(token_ref)
    done(reads)
    ff, d = whole.shape
    height = ff // 4
    waits = []
    for i in range(4):
        here = slice(i * height, (i + 1) * height)
        whole[here, :] = tn(hidden_ref[:, here], low_ref[...]).astype(BF)
        if fast:
            copies = tile_copies(
                meta, whole, outs, sems.at[i], [2 * i, 2 * i + 1], [0, 1], ff // 8, 0, ff // 16,
                d // 2,
            )
            go(copies)
            waits += tile_waits(whole, outs, sems.at[i], 4, 0, ff // 16, d // 2)
    if not fast:
        waits = [pltpu.make_async_copy(whole, outs[0], sems.at[0, 0])]
        go(waits)
    done(waits + ahead)


def up_grad(fast, meta, hidden, low, wu, others, deps=()):
    n, d = low.shape
    ff = hidden.shape[1]
    shapes = grad_shapes(fast, ff, d)
    return kernel_call(
        functools.partial(up_grad_kernel, fast),
        deps,
        [SMEM, WHOLE] + [ANY] * 6,
        [meta, near(hidden), far(low), far(wu), *map(far, others)],
        out_specs=[WHOLE, ANY][-len(shapes) :] + [WHOLE] * 7,
        out_shape=shapes
        + [TOKEN, VMEM((n, ff), BF), VMEM((ff, d), BF)]
        + [VMEM(v.shape, v.dtype) for v in others],
        scratch_shapes=[
            pltpu.VMEM((n, d), BF),
            pltpu.VMEM((ff, d), BF),
            pltpu.SemaphoreType.DMA((4, 8)),
            pltpu.SemaphoreType.DMA((5,)),
            pltpu.SemaphoreType.DMA((32,)),
        ],
        input_output_aliases={1: len(shapes) + 1},
        cost_estimate=pl.CostEstimate(
            flops=4 * n * d * ff, bytes_accessed=2 * n * ff, transcendentals=0
        ),
        mebibytes=12,
        name="up_grad",
    )


def first_back_kernel(*refs):
    second_ref, hidden_ref, wu_ref, xhat_ref, rstd_ref, wo_ref, gain_ref = refs[:7]
    sum_far, low_far, mix_ref, sums_ref, sum_ref, low_ref, sem = refs[7:]
    n, d = low_ref.shape
    tile = 256
    count = n // tile
    writes = []
    for i in range(count):
        part = pl.ds(i * tile, tile)
        writes.append(
            [
                pltpu.make_async_copy(sum_ref.at[part], sum_far.at[part], sem.at[0, i]),
                pltpu.make_async_copy(low_ref.at[part], low_far.at[part], sem.at[1, i]),
            ]
        )
    product = nn(hidden_ref[:tile, :], wu_ref[...])
    sums = [jnp.zeros((1, d), F32)] * 3
    for i in range(count):
        part = slice(i * tile, (i + 1) * tile)
        if i:
            go(writes[i - 1])
        grad = second_ref[part, :] + product
        if i + 1 < count:
            product = nn(hidden_ref[(i + 1) * tile : (i + 2) * tile, :], wu_ref[...])
        xhat = xhat_ref[part, :]
        attn_sum = norm_back(grad, xhat, rstd_ref[part, :1], gain_ref[...])
        sum_ref[part, :] = attn_sum
        low = attn_sum.astype(BF)
        low_ref[part, :] = low
        mix_ref[part, :] = nn(low, wo_ref[...]).astype(BF)
        for k, value in enumerate((grad * xhat, grad, low.astype(F32))):
            sums[k] = sums[k] + jnp.sum(value, axis=0, keepdims=True)
    go(writes[-1])
    for k in range(3):
        sums_ref[k : k + 1, :] = sums[k]
    for group in writes:
        done(group)


def first_back(second, hidden, wu, xhat, rstd, wo, gain, deps=()):
    n, ff = hidden.shape
    d = xhat.shape[1]
    return kernel_call(
        first_back_kernel,
        deps,
        [WHOLE] * 7,
        [near(v) for v in (second, hidden, wu, xhat, rstd, wo)] + [gain],
        out_specs=[ANY, ANY, WHOLE, WHOLE],
        out_shape=[
            HBM((n, d), F32),
            HBM((n, d), BF),
            VMEM((n, d), BF),
            jax.ShapeDtypeStruct((8, d), F32),
        ],
        scratch_shapes=[
            pltpu.VMEM((n, d), F32),
            pltpu.VMEM((n, d), BF),
            pltpu.SemaphoreType.DMA((2, n // 256)),
        ],
        cost_estimate=pl.CostEstimate(
            flops=4 * n * d * ff, bytes_accessed=2 * n * ff, transcendentals=0
        ),
        mebibytes=12,
        name="first_back",
    )


def attention_back_kernel(seq, *refs):
    mix_ref, joined_ref, probs_ref, grad_ref, sums_ref = refs
    d = mix_ref.shape[1]

    @pl.when(pl.program_id(0) == 0)
    def _():
        sums_ref[...] = jnp.zeros_like(sums_ref)

    for p in range(mix_ref.shape[0] // seq):
        here = pl.ds(p * seq, seq)
        for h in range(d // 128):
            one = pl.ds(h * 128, 128)
            two = pl.ds(d + h * 128, 128)
            three = pl.ds(2 * d + h * 128, 128)
            outer = split_heads(mix_ref[here, one])
            probs = probs_ref[p, h]
            grad_probs = nt(joined_ref[here, three], outer)
            wide = probs.astype(F32)
            product = wide * grad_probs
            scores = product - wide * jnp.sum(product, axis=0, keepdims=True)
            scores = scores.astype(BF)
            grad_ref[here, three] = nn(probs, outer).astype(BF)
            grad_ref[here, two] = nn(scores, split_heads(joined_ref[here, one])).astype(BF)
            keys = split_heads(joined_ref[here, two])
            grad_ref[here, one] = (nn(turn_heads(scores), keys) * 0.125).astype(BF)
    sums_ref[0:1, :] += jnp.sum(grad_ref[:, :d].astype(F32), axis=0, keepdims=True)
    sums_ref[1:2, :] += jnp.sum(grad_ref[:, 2 * d :].astype(F32), axis=0, keepdims=True)


def attention_back(mix, joined, probs, seq, deps=()):
    n, d = mix.shape
    tile = 2 * seq
    return kernel_call(
        functools.partial(attention_back_kernel, seq),
        deps,
        [
            rows((tile, d)),
            rows((tile, 3 * d)),
            rows((2, d // 128, seq, 2 * seq)),
        ],
        [near(mix), far(joined), far(probs)],
        grid=(n // tile,),
        out_specs=[rows((tile, 3 * d)), fixed((8, d))],
        out_shape=[
            HBM((n, 3 * d), BF),
            jax.ShapeDtypeStruct((8, d), F32),
        ],
        cost_estimate=pl.CostEstimate(
            flops=16 * n * d * d, bytes_accessed=30 * n * d, transcendentals=0
        ),
        mebibytes=14,
        name="attention_back",
    )


def qkv_grad_kernel(fast, *refs):
    meta, grad_far, x_far, low_far, mix_far = refs[:5]
    outs = refs[5:7]
    token_ref, whole, whole_out, grad_ref, x_ref, low_ref, mix_ref, sem_a, sem_b, sem_c = refs[7:]
    total, d = whole.shape
    width = total // 6
    columns = [pl.ds(i * width, width) for i in range(6)]
    reads = [
        pltpu.make_async_copy(x_far, x_ref, sem_c.at[0]),
        pltpu.make_async_copy(low_far, low_ref, sem_c.at[1]),
        pltpu.make_async_copy(mix_far, mix_ref, sem_c.at[2]),
    ]
    grads = [
        pltpu.make_async_copy(grad_far.at[:, here], grad_ref.at[:, here], sem_c.at[3 + i])
        for i, here in enumerate(columns)
    ]
    go(reads[:1] + grads + reads[1:])
    token_ref[...] = jnp.zeros_like(token_ref)
    waits = []
    done(reads[:1])
    for i in range(2):
        for k in range(3 * i, 3 * i + 3):
            done([grads[k]])
            here = slice(k * width, (k + 1) * width)
            whole[here, :] = tn(grad_ref[:, here], x_ref[...]).astype(BF)
        if fast:
            go(
                tile_copies(
                    meta, whole, outs, sem_a.at[i], range(4 * i, 4 * i + 4), [0, 1], total // 8,
                    0, total // 16, d // 2,
                )
            )
            waits += tile_waits(whole, outs, sem_a.at[i], 8, 0, total // 16, d // 2)
    done(reads[1:])
    whole_out[...] = tn(low_ref[...], mix_ref[...]).astype(BF)
    if fast:
        go(
            tile_copies(
                meta, whole_out, outs, sem_b, range(8), [0, 1], d // 8, total // 16, d // 16,
                d // 2,
            )
        )
        waits += tile_waits(whole_out, outs, sem_b, 16, total // 16, d // 16, d // 2)
    else:
        waits = [
            pltpu.make_async_copy(whole, outs[0], sem_b.at[0]),
            pltpu.make_async_copy(whole_out, outs[1], sem_b.at[1]),
        ]
        go(waits)
    done(waits)


def qkv_grad(fast, meta, grad, x, low, mix, deps=()):
    n, d = x.shape
    if fast:
        shapes = [f((16, 4 * d // 16, d // 2), BF) for f in (VMEM, HBM)]
    else:
        shapes = [jax.ShapeDtypeStruct((3 * d, d), BF), jax.ShapeDtypeStruct((d, d), BF)]
    return kernel_call(
        functools.partial(qkv_grad_kernel, fast),
        deps,
        [SMEM, ANY, ANY, ANY, ANY],
        [meta, far(grad), far(x), far(low), far(mix)],
        out_specs=([WHOLE, ANY] if fast else [ANY] * 2) + [WHOLE],
        out_shape=shapes + [TOKEN],
        scratch_shapes=[
            pltpu.VMEM((3 * d, d), BF),
            pltpu.VMEM((d, d), BF),
            pltpu.VMEM((n, 3 * d), BF),
            pltpu.VMEM((n, d), BF),
            pltpu.VMEM((n, d), BF),
            pltpu.VMEM((n, d), BF),
            pltpu.SemaphoreType.DMA((2, 16)),
            pltpu.SemaphoreType.DMA((32,)),
            pltpu.SemaphoreType.DMA((9,)),
        ],
        cost_estimate=pl.CostEstimate(
            flops=16 * n * d * d, bytes_accessed=16 * n * d, transcendentals=0
        ),
        mebibytes=20,
        name="qkv_grad",
    )


def tokens_grad_kernel(sum_ref, grad_ref, w_ref, out_ref, token_ref):
    token_ref[...] = jnp.zeros_like(token_ref)
    out_ref[...] = sum_ref[...] + nn(grad_ref[...], w_ref[...])


def tokens_back(attn_sum, grad, w, deps=()):
    n, d = attn_sum.shape
    tile = 256
    return kernel_call(
        tokens_grad_kernel,
        deps,
        [rows((tile, d)), rows((tile, 3 * d)), fixed((3 * d, d))],
        [far(attn_sum), far(grad), far(w)],
        grid=(n // tile,),
        out_specs=[rows((tile, d)), fixed((8, 128))],
        out_shape=[HBM((n, d), F32), TOKEN],
        cost_estimate=pl.CostEstimate(
            flops=12 * n * d * d, bytes_accessed=14 * n * d, transcendentals=0
        ),
        mebibytes=14,
        name="tokens_back",
    )


AXES = ("rep", "shard")


def route(fn):
    pairs = []
    for x in range(2):
        for c in range(2):
            for z in range(4):
                for y in range(2):
                    to = fn(x, c, z, y)
                    pairs.append(
                        ((x * 2 + c) * 8 + z * 2 + y, (to[0] * 2 + to[1]) * 8 + to[2] * 2 + to[3])
                    )
    return pairs


def to_core(v):
    return lax.ppermute(v, AXES, route(lambda x, c, z, y: (x, 1 - c, z, y)))


def to_x(v):
    return lax.ppermute(v, AXES, route(lambda x, c, z, y: (1 - x, c, z, y)))


def to_z(v, k):
    return lax.ppermute(v, AXES, route(lambda x, c, z, y: (x, c, z ^ k, y)))


def to_cross(v, first_core):
    return lax.ppermute(
        v,
        AXES,
        route(lambda x, c, z, y: (1 - x, c, z, y) if c == first_core else (x, c, z, 1 - y)),
    )


def after(value, *others):
    return lax.optimization_barrier((value, others))[0]


def start_gather(own):
    return jnp.stack([own] + [to_z(own, k) for k in (1, 2, 3)])


def first_cross(along):
    return jnp.concatenate([along, to_cross(along, 0)])


def add_core_kernel(kept_ref, got_ref, *refs):
    keep_ref, send_ref = refs[-2:]
    count, height, width = keep_ref.shape
    for k in range(count):
        here = slice(k * height, (k + 1) * height)
        keep_ref[k] = (kept_ref[k].astype(F32) + got_ref[k].astype(F32)).astype(BF)
        other = kept_ref[count + k].astype(F32) + got_ref[count + k].astype(F32)
        send_ref[here, :] = other.astype(BF)
    if len(refs) == 3:
        send_ref[count * height :, :] = refs[0][...].astype(BF)


def add_cross_kernel(keep_ref, got_ref, *refs):
    small = len(refs) == 4
    new_ref, send_ref = refs[1:3] if small else refs
    count, height, width = new_ref.shape
    for k in range(2 * count):
        here = slice(k * height, (k + 1) * height)
        total = (keep_ref[k].astype(F32) + got_ref[here, :].astype(F32)).astype(BF)
        if k < count:
            new_ref[k] = total
        else:
            send_ref[(k - count) * height : (k - count + 1) * height, :] = total
    if small:
        rows_in = refs[0][...] + got_ref[2 * count * height :, :].astype(F32)
        refs[3][...] = rows_in
        tail = jnp.concatenate([rows_in[count : 2 * count], rows_in[2 * count :]], axis=0)
        tail = jnp.concatenate([tail, jnp.zeros((count, width), F32)], axis=0)
        send_ref[count * height :, :] = tail.astype(BF)


def add_last_kernel(keep_ref, got_ref, *refs):
    small = len(refs) == 5
    outs = refs[1:] if small else refs
    count, height, width = keep_ref.shape
    if small:
        rows_in = refs[0][...] + got_ref[count * height :, :].astype(F32)
        place = lax.broadcasted_iota(jnp.int32, rows_in.shape, 0)
    for k in range(count):
        here = slice(k * height, (k + 1) * height)
        total = keep_ref[k].astype(F32) + got_ref[here, :].astype(F32)
        outs[k][:height, :] = total.astype(outs[k].dtype)
        if small:
            row = jnp.sum(jnp.where(place == k, rows_in, 0.0), axis=0, keepdims=True)
            outs[k][height:, :] = jnp.broadcast_to(row, (16, width)).astype(outs[k].dtype)


def total_kernel(own_ref, one_ref, two_ref, three_ref, out_ref):
    total = own_ref[...] + one_ref[...].astype(F32)
    total = total + two_ref[...].astype(F32) + three_ref[...].astype(F32)
    out_ref[...] = total.astype(BF)


class Scatter:
    def __init__(self, kept, sent):
        self.kept, self.small = kept, None
        self.got = to_core(sent)

    def call(self, body, out_shape, extra, deps, name):
        args = [near(self.keep), near(self.got)] + list(extra)

        def marked(*refs):
            refs[-1][...] = jnp.zeros_like(refs[-1])
            body(*refs[:-1])

        *out, self.token = kernel_call(
            marked,
            deps,
            [WHOLE] * len(args),
            args,
            out_specs=[WHOLE] * (len(out_shape) + 1),
            out_shape=out_shape + [TOKEN],
            name=name,
        )
        return out

    def add_core(self, deps=(), small=None):
        self.keep = self.kept
        count, height, width = self.kept.shape[0] // 2, *self.kept.shape[1:]
        tail, extra = 0, []
        if small is not None:
            tail, extra = 16, [jnp.concatenate([small[8:], jnp.zeros_like(small[8:])])]
            self.small = jnp.concatenate([small[:8], jnp.zeros_like(small[8:])])
        self.keep, self.send = self.call(
            add_core_kernel,
            [VMEM((count, height, width), BF), VMEM((count * height + tail, width), BF)],
            extra,
            deps,
            "add_core",
        )
        return self.token

    def cross(self, core):
        self.got = to_cross(self.send, core)

    def add_cross(self, deps=()):
        count, height, width = self.keep.shape[0] // 2, *self.keep.shape[1:]
        small = self.small is not None
        outs = [
            VMEM((count, height, width), BF),
            VMEM((count * height + 16 * small, width), BF),
        ]
        if small:
            outs.append(VMEM((16, width), F32))
        out = self.call(
            add_cross_kernel, outs, [self.small] if small else [], deps, "add_cross"
        )
        self.keep, self.send = out[:2]
        if small:
            self.small = out[2]
        return self.token

    def add_last(self, deps=()):
        height, width = self.keep.shape[1:]
        small = self.small is not None
        shape = (height + 16 * small, width)
        self.parts = self.call(
            add_last_kernel,
            [VMEM(shape, F32)] + [VMEM(shape, BF)] * 3,
            [self.small] if small else [],
            deps,
            "add_last",
        )
        return self.token

    def along(self):
        self.got = [to_z(self.parts[k], k) for k in (1, 2, 3)]

    def total(self, deps=()):
        args = [near(v) for v in [self.parts[0]] + self.got]
        return kernel_call(
            total_kernel,
            deps,
            [WHOLE] * 4,
            args,
            out_specs=WHOLE,
            out_shape=jax.ShapeDtypeStruct(self.parts[0].shape, BF),
            name="total",
        )


def finish_kernel(meta, mine_ref, other_ref, qkv_ref, out_ref, small_ref):
    c = meta[1]
    first = 0
    for target in (qkv_ref, out_ref):
        half = target.shape[0] // 2
        part = slice(first, first + half)
        target[pl.ds(pl.multiple_of(c * half, 8), half), :] = mine_ref[part, :].astype(F32)
        target[pl.ds(pl.multiple_of((1 - c) * half, 8), half), :] = other_ref[part, :].astype(F32)
        first += half
    mine = mine_ref[first : first + 16, :].astype(F32)[:1]
    other = other_ref[first : first + 16, :].astype(F32)[:1]
    width = small_ref.shape[1]
    for k, line in enumerate((jnp.where(c == 0, mine, other), jnp.where(c == 0, other, mine))):
        small_ref[2 * k : 2 * k + 1, :] = line[:, :width]
        small_ref[2 * k + 1 : 2 * k + 2, :] = line[:, width:]


def finish(meta, mine, other, d):
    return kernel_call(
        finish_kernel,
        [],
        [SMEM, WHOLE, WHOLE],
        [meta, near(mine), near(other)],
        out_specs=[WHOLE] * 3,
        out_shape=[HBM((3 * d // 8, d), F32), HBM((d // 8, d), F32), VMEM((4, d // 2), F32)],
        name="finish",
    )


def in_columns(piece):
    return jnp.concatenate(jnp.split(piece, 4, axis=0), axis=1)


def side_by_side(low, across, x):
    return jnp.concatenate(
        [jnp.where(x == 0, low, across), jnp.where(x == 0, across, low)], axis=1
    )


def owner_block(mine, other, c, first, height):
    mine, other = mine[first : first + height], other[first : first + height]
    return jnp.concatenate(
        [jnp.where(c == 0, mine, other), jnp.where(c == 0, other, mine)], axis=0
    ).astype(F32)


def quarter_of(w, x, c):
    half_rows, half_cols = w.shape[0] // 2, w.shape[1] // 2
    side = jnp.where(x == 0, w[:, :half_cols], w[:, half_cols:])
    return jnp.where(c == 0, side[:half_rows], side[half_rows:]).astype(BF)


def order_matrix(x, c, z, y):
    rel = jnp.arange(32, dtype=jnp.int32)
    other, a, b, rz = rel // 16, rel // 8 % 2, rel // 4 % 2, rel % 4
    cc = c ^ other
    y_rel = jnp.where(cc == 0, a, b)
    x_rel = jnp.where(cc == 0, b, a)
    place = (((z ^ rz) * 2 + (y ^ y_rel)) * 2 + cc) * 2 + (x ^ x_rel)
    return (place[:, None] == rel[None, :]).astype(F32)


def line_tables(heights):
    place = []
    for shard in range(8):
        at = 0
        for height in heights:
            place += [at + shard * height + k for k in range(height)]
            at += 8 * height
    place = np.array(place).reshape(32, -1)
    count = place.size // 8
    row = np.zeros((place.shape[1], 32, 16), np.float32)
    lane = np.zeros((place.shape[1], 32, 8), np.float32)
    for piece in range(32):
        for k in range(place.shape[1]):
            row[k, piece, place[piece, k] // 8] = 1.0
            lane[k, piece, place[piece, k] % 8] = 1.0
    assert count <= 16
    return jnp.asarray(row), jnp.asarray(lane)


def pack_kernel(order, rows_of, lanes_of, attn_ref, first_ref, bias_ref, two_ref, keep_ref, send_ref, vecs):
    d = vecs.shape[1]
    width = d // 8
    vecs[...] = jnp.zeros_like(vecs)
    vecs[0:2, :] = attn_ref[0:2, :]
    vecs[2:3, :] = first_ref[2:3, :]
    vecs[3:5, :] = first_ref[0:2, :]
    for k in range(4):
        vecs[5 + k : 6 + k, :] = bias_ref[:, k * d : (k + 1) * d]
    vecs[9:10, :] = two_ref[2:3, :]
    vecs[10:12, :] = two_ref[0:2, :]
    parts = []
    for k in range(rows_of.shape[0]):
        chosen = jnp.dot(
            rows_of[k], vecs[...], preferred_element_type=F32, precision=lax.Precision.HIGHEST
        )
        part = jnp.zeros((32, width), F32)
        for m in range(8):
            part = part + chosen[:, m * width : (m + 1) * width] * lanes_of[k, :, m : m + 1]
        parts.append(part)
    parts.append(jnp.zeros((32, keep_ref.shape[1] - len(parts) * width), F32))
    packed = jnp.concatenate(parts, axis=1)
    packed = jnp.dot(
        order[...], packed, preferred_element_type=F32, precision=lax.Precision.HIGHEST
    )
    keep_ref[...] = packed[:16]
    send_ref[...] = packed[16:].astype(BF)


def pack_small(order, tables, attn, first, bias, two):
    d = attn.shape[1]
    return kernel_call(
        pack_kernel,
        [],
        [WHOLE] * 7,
        [order, *tables, attn, first, bias, two],
        out_specs=[WHOLE] * 2,
        out_shape=[
            jax.ShapeDtypeStruct((16, d // 2), F32),
            jax.ShapeDtypeStruct((16, d // 2), BF),
        ],
        scratch_shapes=[pltpu.VMEM((16, d), F32)],
        name="pack_small",
    )


def per_device(
    tokens,
    word_counts,
    region_counts,
    qkv_weight,
    qkv_bias,
    out_weight,
    out_bias,
    attn_gain,
    attn_shift,
    up_weight,
    up_bias,
    down_weight,
    down_bias,
    ffn_gain,
    ffn_shift,
    cotangent,
):
    pairs, seq, d = tokens.shape
    n = pairs * seq
    shard_count, rep_count = lax.axis_size("shard"), lax.axis_size("rep")
    fast = shard_count == 8 and rep_count == 4
    rep, shard = lax.axis_index("rep"), lax.axis_index("shard")
    x, c, z, y = rep // 2, rep % 2, shard // 2, shard % 2
    meta = jnp.stack([x, c, z, y]).astype(jnp.int32)
    vectors = (qkv_bias, out_bias, attn_gain, attn_shift, up_bias, down_bias, ffn_gain, ffn_shift)
    small_own = jnp.concatenate(vectors)
    sizes = [v.shape[0] for v in vectors]

    flat = tokens.reshape(n, d)
    if fast:
        quarter = small_own.shape[0] // 4
        own_small = jnp.where(
            x == 0,
            jnp.where(c == 0, small_own[:quarter], small_own[2 * quarter : 3 * quarter]),
            jnp.where(c == 0, small_own[quarter : 2 * quarter], small_own[3 * quarter :]),
        )
        own_small = jnp.pad(own_small.astype(BF)[None, :], ((0, 15), (0, d // 2 - quarter)))
        own_one = jnp.concatenate(
            [quarter_of(qkv_weight, x, c), quarter_of(out_weight, x, c), own_small], axis=0
        )
        up_pieces = [lax.all_gather(quarter_of(up_weight, x, c), AXES, axis=0)]
        along_one = start_gather(own_one)
        eight_one = first_cross(along_one)
        more_one = to_cross(eight_one, 1)
        along_two = start_gather(after(quarter_of(down_weight, x, c), eight_one))
        other_one = to_core(eight_one)
        along_two, more_one, other_one = after((along_two, more_one, other_one))
        last_one = to_core(more_one)
        qkv_pieces = [eight_one, more_one, other_one, last_one]
        order = order_matrix(x, c, z, y)
        row = d // 4
        tables = line_tables([v // (d // 8) for v in sizes])
        rel_small = jnp.concatenate([p[:, row, :quarter] for p in qkv_pieces]).astype(F32)
        whole_small = lax.dot_general(
            order, rel_small, (((0,), (0,)), ((), ())), precision=lax.Precision.HIGHEST
        ).reshape(8, -1)
        cross_two = to_cross(along_two, 0)
        first_deps = [along_two]
    else:
        qkv_pieces = [
            lax.all_gather(w.astype(BF), "shard", axis=0, tiled=True)
            for w in (qkv_weight, out_weight)
        ]
        whole_small = lax.all_gather(small_own.astype(BF), "shard", axis=0).astype(F32)
        first_deps = []
    parts, at = [], 0
    for size in sizes:
        parts.append(whole_small[:, at : at + size].reshape(1, -1))
        at += size
    bqv, bo, g1, c1, bu, bd, g2, c2 = parts

    vec_one = jnp.concatenate([bqv, bo, g1, c1], axis=1)
    vec_two = jnp.concatenate([g1, c1, bd, g2, c2], axis=1)
    joined, probs, mix, low, xhat, rstd, wqkv, wo = attention_forward(
        fast, meta, word_counts, region_counts, flat, vec_one, qkv_pieces, seq, first_deps
    )
    if fast:
        cross_two = after(cross_two, rstd)
        eight_two = jnp.concatenate([along_two, cross_two])
        more_two = to_cross(eight_two, 1)
        up_deps = [eight_two, vec_two]
    else:
        up_pieces = [lax.all_gather(up_weight.astype(BF), "shard", axis=0, tiled=True)]
        up_deps = []
    act, slope, token = up_forward(fast, meta, low, bu, up_pieces, up_deps)
    if fast:
        more_two = after(more_two, token)
        down_pieces = [eight_two, more_two, to_core(after(eight_two, token)), to_core(more_two)]
    else:
        down_pieces = [lax.all_gather(down_weight.astype(BF), "shard", axis=0, tiled=True)]
    layer_out, second, feed, sums_two, wd, slope, *down_grads = down_forward(
        fast, meta, word_counts, region_counts, act, slope, xhat, vec_two,
        cotangent.reshape(n, d), down_pieces, seq,
    )
    deps = []
    if fast:
        down_sum = Scatter(*down_grads)
    hidden, grad_bu = hidden_grad(feed, slope, wd)
    if fast:
        deps = [down_sum.add_core([grad_bu])]
        down_sum.cross(1)
    up_out = up_grad(fast, meta, hidden, low, up_pieces[0], [second, xhat, rstd, wo], deps)
    up_grads, (token, hidden, wu, second, xhat, rstd, wo) = up_out[:-7], up_out[-7:]
    deps = [token]
    if fast:
        deps = [down_sum.add_cross([token])]
        up_sum = Scatter(up_grads[0], after(up_grads[1], deps[0]))
        down_sum.cross(0)
    attn_sum, attn_low, grad_mix, sums_first = first_back(
        second, hidden, wu, xhat, rstd, wo, g1, deps
    )
    if fast:
        deps = [down_sum.add_last([sums_first]), up_sum.add_core([sums_first])]
        down_sum.along()
        up_sum.cross(1)
    grad_joined, sums_attn = attention_back(grad_mix, joined, probs, seq, deps)
    grad_vectors = [
        jnp.concatenate([sums_attn[0:1], sums_attn[1:2]], axis=1),
        sums_first[2:3],
        sums_first[0:1],
        sums_first[1:2],
        grad_bu,
        sums_two[2:3],
        sums_two[0:1],
        sums_two[1:2],
    ]
    deps = []
    if fast:
        small, small_low = pack_small(order, tables, sums_attn, sums_first, grad_bu, sums_two)
        deps = [up_sum.add_cross([sums_attn]), small_low] + down_sum.got
        up_sum.cross(0)
        small_got = to_core(small_low)
    qkv_out = qkv_grad(fast, meta, grad_joined, flat, attn_low, mix, deps)
    qkv_grads, token = qkv_out[:2], qkv_out[2]
    if fast:
        small_got, up_sum.got = after((small_got, up_sum.got), token)
        qkv_sum = Scatter(qkv_grads[0], after(qkv_grads[1], small_got, up_sum.got))
        up_sum.add_last()
        up_sum.along()
        small = small + small_got.astype(F32)
        token = qkv_sum.add_core([up_sum.token], small=small)
        qkv_sum.cross(1)
        down_total = down_sum.total([token])
        down_across = to_x(down_total)
        tokens_grad, token = tokens_back(attn_sum, grad_joined, wqkv, [token, down_total])
        token = qkv_sum.add_cross([token, down_across] + up_sum.got)
        qkv_sum.cross(0)
        up_total = up_sum.total([token])
        up_across = to_x(up_total)
        token = qkv_sum.add_last([up_across])
        qkv_sum.along()
        down_mine = side_by_side(in_columns(down_total), in_columns(down_across), x)
        up_mine = side_by_side(up_total, up_across, x)
        down_other, up_other = to_core(down_mine), to_core(up_mine)
        grad_down = owner_block(down_mine, down_other, c, 0, down_mine.shape[0])
        grad_up = owner_block(up_mine, up_other, c, 0, up_mine.shape[0])
        grad_up, grad_down, qkv_sum.got = after((grad_up, grad_down, qkv_sum.got))
        qkv_total = qkv_sum.total()
        qkv_mine = side_by_side(qkv_total, to_x(qkv_total), x)
        qkv_other = to_core(qkv_mine)
        grad_qkv, grad_out, small_all = finish(meta, qkv_mine, qkv_other, d)
        small_total = small_all[:, :quarter].reshape(-1)
    else:
        tokens_grad, _ = tokens_back(attn_sum, grad_joined, wqkv)

        def total(v):
            part = lax.psum_scatter(v.astype(F32), "shard", scatter_dimension=0, tiled=True)
            return lax.psum(part, "rep")

        grad_down, grad_up = total(down_grads[0]), total(up_grads[0])
        grad_qkv, grad_out = total(qkv_grads[0]), total(qkv_grads[1])
        small_total = lax.dynamic_index_in_dim(
            jnp.concatenate(
                [lax.psum(g, AXES).reshape(shard_count, -1) for g in grad_vectors], axis=1
            ),
            shard,
            axis=0,
            keepdims=False,
        )
    vector_grads, at = [], 0
    for size in sizes:
        vector_grads.append(small_total[at : at + size])
        at += size
    g_qv, g_bo, g_g1, g_c1, g_bu, g_bd, g_g2, g_c2 = vector_grads
    return (
        layer_out.reshape(tokens.shape),
        tokens_grad.reshape(tokens.shape),
        grad_qkv,
        g_qv,
        grad_out,
        g_bo,
        g_g1,
        g_c1,
        grad_up,
        g_bu,
        grad_down,
        g_bd,
        g_g2,
        g_c2,
    )


def solution(mesh):
    matrix, vector = P("shard", None), P("shard")
    batch, counts = P(AXES, None, None), P(AXES)
    weights = (
        matrix, vector, matrix, vector, vector, vector,
        matrix, vector, matrix, vector, vector, vector,
    )
    return jax.shard_map(
        per_device,
        mesh=mesh,
        in_specs=(batch, counts, counts) + weights + (batch,),
        out_specs=(batch, batch) + weights,
        check_vma=False,
    )
```

profile of v0, /device:TPU:0, one launch (start us, length us, event | category | flops | bytes accessed | tf_op | source)
XLA Modules:
  0.0 263.6 jit_solution(11749052340849096095)
XLA Ops:
  7.4 1.4 slice_select_fusion
  9.9 3.1 %collective-permute-start = (bf16[208,384]{1,0:T(8,128)(2,1)S(1)}, bf16[208,384]{1,0:T(8,128)(2,1)S(1)}, u32[]{:S(2)}, u32[]{:S(2)}) collective-permute-start(bf16[208,384]{1,0:T(8,128)(2,1)S(1)} %get-tuple-element.215), channel_id=1, source_target_pairs={{0,2},{1,3},{2,0},{3,1},{4,6},{5,7},{6,4},{7,5},{8,10},{9,11},{10,... | collective-permute-start | bytes 479240 | tf_op jit(solution)/shard_map/ppermute | solution.py:841
  13.0 2.6 collective-permute-start.1
  15.6 3.9 %collective-permute-done = bf16[208,384]{1,0:T(8,128)(2,1)S(1)} collective-permute-done((bf16[208,384]{1,0:T(8,128)(2,1)S(1)}, bf16[208,384]{1,0:T(8,128)(2,1)S(1)}, u32[]{:S(2)}, u32[]{:S(2)}) %collective-permute-start) | collective-permute-done | bytes 159776 | tf_op jit(solution)/shard_map/ppermute | solution.py:841
  19.4 9.4 %collective-permute-done.1 = bf16[208,384]{1,0:T(8,128)(2,1)S(1)} collective-permute-done((bf16[208,384]{1,0:T(8,128)(2,1)S(1)}, bf16[208,384]{1,0:T(8,128)(2,1)S(1)}, u32[]{:S(2)}, u32[]{:S(2)}) %collective-permute-start.1) | collective-permute-done | bytes 159776 | tf_op jit(solution)/shard_map/ppermute | solution.py:841
  28.9 1.6 collective-permute-start.3
  30.6 10.4 %collective-permute-done.3 = bf16[4,208,384]{2,1,0:T(8,128)(2,1)S(1)} collective-permute-done((bf16[4,208,384]{2,1,0:T(8,128)(2,1)S(1)}, bf16[4,208,384]{2,1,0:T(8,128)(2,1)S(1)}, u32[]{:S(2)}, u32[]{:S(2)}) %collective-permute-start.3) | collective-permute-done | bytes 639008 | tf_op jit(solution)/shard_map/ppermute | solution.py:845
  41.1 1.6 collective-permute-start.7
  42.8 2.5 collective-permute-start.4
  45.3 1.8 collective-permute-start.5
  47.1 1.4 collective-permute-start.6
  48.5 8.2 %collective-permute-done.4 = bf16[48,1536]{1,0:T(8,128)(2,1)S(1)} collective-permute-done((bf16[48,1536]{1,0:T(8,128)(2,1)S(1)}, bf16[48,1536]{1,0:T(8,128)(2,1)S(1)}, u32[]{:S(2)}, u32[]{:S(2)}) %collective-permute-start.4) | collective-permute-done | bytes 147488 | tf_op jit(solution)/shard_map/ppermute | solution.py:841
  57.2 5.0 %collective-permute-done.6 = bf16[48,1536]{1,0:T(8,128)(2,1)S(1)} collective-permute-done((bf16[48,1536]{1,0:T(8,128)(2,1)S(1)}, bf16[48,1536]{1,0:T(8,128)(2,1)S(1)}, u32[]{:S(2)}, u32[]{:S(2)}) %collective-permute-start.6) | collective-permute-done | bytes 147488 | tf_op jit(solution)/shard_map/ppermute | solution.py:841
  63.5 2.0 collective-permute-start.10
  67.5 18.5 %attention_forward.1 = (bf16[1024,2304]{1,0:T(8,128)(2,1)}, bf16[8,6,128,256]{3,2,1,0:T(8,128)(2,1)}, bf16[1024,768]{1,0:T(8,128)(2,1)}, bf16[1024,768]{1,0:T(8,...) custom-call(s32[4]{0:T(128)S(1)} %pad_add_fusion.refs_0_, ...), custom_call_target="tpu_custom_call" | custom-call | flops 4831838208 | bytes 12582912 | tf_op jit(solution)/shard_map/attention_forward/pallas_call | solution.py:62
  86.9 3.0 %all-gather.3.cloned.1.call-done = bf16[6144,384]{1,0:T(8,128)(2,1)} async-done(((bf16[192,384]{1,0:T(8,128)(2,1)}), bf16[6144,384]{1,0:T(8,128)(2,1)}) %all-gather.3.cloned.1.call-update) | async-done | bytes 4718608 | tf_op jit(solution)/shard_map/all_gather | solution.py:1173
  90.0 12.4 %up_forward.1 = (bf16[1024,3072]{1,0:T(8,128)(2,1)S(1)}, bf16[1024,3072]{1,0:T(8,128)(2,1)S(1)}, f32[8,128]{1,0:T(8,128)}) custom-call(s32[4]{0:T(128)S(1)} %pad_add_fusion.refs_0_, bf16[1024,768]{1,0:T(8,128)(2,1)} %get-tuple-element.112.refs_1_.refs_2_, f32[1,3072]{1,0:T(1,128)S(1)} %bitcast.37, bf16[32,192,384]{2,1,0:T(8,128)(2,1)} %bitcast.48, ...), custom_call_target="tpu_custom_call" | custom-call | flops 9663676416 | bytes 12582912 | tf_op jit(solution)/shard_map/up_forward/pallas_call | solution.py:62
  103.0 2.3 collective-permute-done.12.refs_10_
  105.3 1.9 collective-permute-done.13.refs_11_
  107.2 20.5 %down_forward.1 = (bf16[1024,768]{1,0:T(8,128)(2,1)}, f32[1024,768]{1,0:T(8,128)}, bf16[1024,768]{1,0:T(8,128)(2,1)S(1)}, f32[8,768]{1,0:T(8,128)S(1)}, bf16[768...) custom-call(s32[4]{0:T(128)S(1)} %pad_add_fusion.refs_0_, ...), custom_call_target="tpu_custom_call", output_to_operand_aliasing={{5}: (4, {})} | custom-call | flops 28991029248 | bytes 6291456 | tf_op jit(solution)/shard_map/down_forward/pallas_call | solution.py:62
  128.1 5.4 %hidden_grad.1 = (bf16[1024,3072]{1,0:T(8,128)(2,1)S(1)}, f32[1,3072]{1,0:T(1,128)S(1)}) custom-call(bf16[1024,768]{1,0:T(8,128)(2,1)S(1)} %get-tuple-element.122.refs_0_, bf16[1024,3072]{1,0:T(8,128)(2,1)S(1)} %get-tuple-element.123.refs_1_, bf16[768,3072]{1,0:T(8,128)(2,1)S(1)} %get-tuple-element.124.refs_2_), custom_call_target="tpu_custom_call" | custom-call | flops 9663676416 | bytes 12582912 | tf_op jit(solution)/shard_map/hidden_grad/pallas_call | solution.py:62
  134.0 2.3 collective-permute-start.15
  136.4 10.0 %up_grad.1 = (bf16[16,192,384]{2,1,0:T(8,128)(2,1)S(1)}, bf16[16,192,384]{2,1,0:T(8,128)(2,1)}, f32[8,128]{1,0:T(8,128)S(1)}, bf16[1024,3072]{1,0:T(8,128)(2,1)S...) custom-call(s32[4]{0:T(128)S(1)} %pad_add_fusion.refs_0_, ...), custom_call_target="tpu_custom_call", output_to_operand_aliasing={{3}: (1, {})} | custom-call | flops 9663676416 | bytes 6291456 | tf_op jit(solution)/shard_map/up_grad/pallas_call | solution.py:62
  146.4 4.2 %collective-permute-done.15.refs_1_ = bf16[1536,384]{1,0:T(8,128)(2,1)S(1)} collective-permute-done((bf16[1536,384]{1,0:T(8,128)(2,1)S(1)}, bf16[1536,384]{1,0:T(8,128)(2,1)S(1)}, u32[]{:S(2)}, u32[]{:S(2)}) %collective-permute-start.15) | collective-permute-done | bytes 1179680 | tf_op jit(solution)/shard_map/ppermute | solution.py:845
  150.9 1.5 collective-permute-start.16
  152.5 9.0 %first_back.1 = (f32[1024,768]{1,0:T(8,128)}, bf16[1024,768]{1,0:T(8,128)(2,1)}, bf16[1024,768]{1,0:T(8,128)(2,1)S(1)}, f32[8,768]{1,0:T(8,128)S(1)}) custom-call(f32[1024,768]{1,0:T(8,128)S(1)} %get-tuple-element.132.refs_0_, bf16[1024,3072]{1,0:T(8,128)(2,1)S(1)} %get-tuple-element.133.refs_1_, bf16[3072,768]{1,0:T(8,128)(2,1)S(1)} %get-tuple-element.134.refs_2_, ...), custom_call_target="tpu_custom_call" | custom-call | flops 9663676416 | bytes 6291456 | tf_op jit(solution)/shard_map/first_back/pallas_call | solution.py:62
  162.9 1.9 collective-permute-start.19
  165.5 1.9 collective-permute-start.21
  167.4 13.1 %attention_back.1 = (bf16[1024,2304]{1,0:T(8,128)(2,1)}, f32[8,768]{1,0:T(8,128)S(1)}) custom-call(bf16[1024,768]{1,0:T(8,128)(2,1)S(1)} %get-tuple-element.143.refs_0_, bf16[1024,2304]{1,0:T(8,128)(2,1)} %get-tuple-element.144.refs_1_, bf16[8,6,128,256]{3,2,1,0:T(8,128)(2,1)} %get-tuple-element.145.refs_2_, f32[8,128]{1,0:T(8,128)S(1)} %get-tuple-element.149.refs_3_, ...), custom_call_target="tpu_custom_call" | custom-call | flops 9663676416 | bytes 23592960 | tf_op jit(solution)/shard_map/attention_back/pallas_call | solution.py:62
  181.6 2.1 collective-permute-start.23
  183.7 11.9 %qkv_grad.1 = (bf16[16,192,384]{2,1,0:T(8,128)(2,1)S(1)}, bf16[16,192,384]{2,1,0:T(8,128)(2,1)}, f32[8,128]{1,0:T(8,128)}) custom-call(s32[4]{0:T(128)S(1)} %pad_add_fusion.refs_0_, bf16[1024,2304]{1,0:T(8,128)(2,1)} %get-tuple-element.154.refs_1_, bf16[1024,768]{1,0:T(8,128)(2,1)} %bitcast.52, bf16[1024,768]{1,0:T(8,128)(2,1)} %get-tuple-element.156.refs_3_, ...), custom_call_target="tpu_custom_call" | custom-call | flops 9663676416 | bytes 12582912 | tf_op jit(solution)/shard_map/qkv_grad/pallas_call | solution.py:62
  196.1 1.8 collective-permute-start.28
  197.9 2.4 collective-permute-start.29
  201.6 1.7 collective-permute-start.25
  203.3 4.5 %collective-permute-done.26.refs_4_ = bf16[192,384]{1,0:T(8,128)(2,1)S(1)} collective-permute-done((bf16[192,384]{1,0:T(8,128)(2,1)S(1)}, bf16[192,384]{1,0:T(8,128)(2,1)S(1)}, u32[]{:S(2)}, u32[]{:S(2)}) %collective-permute-start.26) | collective-permute-done | bytes 147488 | tf_op jit(solution)/shard_map/ppermute | solution.py:837
  208.0 9.0 %tokens_back.1 = (f32[1024,768]{1,0:T(8,128)}, f32[8,128]{1,0:T(8,128)S(1)}) custom-call(f32[1024,768]{1,0:T(8,128)} %get-tuple-element.142.refs_0_, bf16[1024,2304]{1,0:T(8,128)(2,1)} %get-tuple-element.154.refs_1_, bf16[2304,768]{1,0:T(8,128)(2,1)} %get-tuple-element.155.refs_2_, f32[8,128]{1,0:T(8,128)S(1)} %get-tuple-element.176.refs_4_.refs_3_, ...), custom_call_target="tpu_custom_call" | custom-call | flops 7247757312 | bytes 11010048 | tf_op jit(solution)/shard_map/tokens_back/pallas_call | solution.py:62
  218.3 1.7 collective-permute-start.31
  220.6 3.8 %collective-permute-done.31.refs_3_ = bf16[192,384]{1,0:T(8,128)(2,1)S(1)} collective-permute-done((bf16[192,384]{1,0:T(8,128)(2,1)S(1)}, bf16[192,384]{1,0:T(8,128)(2,1)S(1)}, u32[]{:S(2)}, u32[]{:S(2)}) %collective-permute-start.31) | collective-permute-done | bytes 147488 | tf_op jit(solution)/shard_map/ppermute | solution.py:837
  224.5 1.6 collective-permute-start.32
  227.2 4.4 %collective-permute-done.30.refs_1_ = bf16[784,384]{1,0:T(8,128)(2,1)S(1)} collective-permute-done((bf16[784,384]{1,0:T(8,128)(2,1)S(1)}, bf16[784,384]{1,0:T(8,128)(2,1)S(1)}, u32[]{:S(2)}, u32[]{:S(2)}) %collective-permute-start.30) | collective-permute-done | bytes 602144 | tf_op jit(solution)/shard_map/ppermute | solution.py:845
  232.7 1.7 collective-permute-start.35
  234.4 2.2 collective-permute-start.36
  237.8 2.2 collective-permute-done.34.refs_1_
  240.0 5.9 %collective-permute-done.35.refs_2_ = bf16[208,384]{1,0:T(8,128)(2,1)S(1)} collective-permute-done((bf16[208,384]{1,0:T(8,128)(2,1)S(1)}, bf16[208,384]{1,0:T(8,128)(2,1)S(1)}, u32[]{:S(2)}, u32[]{:S(2)}) %collective-permute-start.35) | collective-permute-done | bytes 159776 | tf_op jit(solution)/shard_map/ppermute | solution.py:841
  245.9 1.4 collective-permute-start.37
  247.3 4.0 %collective-permute-done.37 = bf16[208,384]{1,0:T(8,128)(2,1)S(1)} collective-permute-done((bf16[208,384]{1,0:T(8,128)(2,1)S(1)}, bf16[208,384]{1,0:T(8,128)(2,1)S(1)}, u32[]{:S(2)}, u32[]{:S(2)}) %collective-permute-start.37) | collective-permute-done | bytes 159776 | tf_op jit(solution)/shard_map/ppermute | solution.py:837
  251.4 1.6 collective-permute-done.38.refs_2_
  253.0 1.6 finish.1
  (167 shorter events, 20.5 us)
Async XLA Ops:
  7.3 82.7 %all-gather.3.cloned.1.call-start = ((), (), s32[]{:S(2)}) async-start(), calls=%async_computation | async-start | bytes 4866048 | tf_op jit(solution)/shard_map/all_gather | solution.py:1173
  9.9 9.6 %collective-permute-start = (bf16[208,384]{1,0:T(8,128)(2,1)S(1)}, bf16[208,384]{1,0:T(8,128)(2,1)S(1)}, u32[]{:S(2)}, u32[]{:S(2)}) collective-permute-start(bf16[208,384]{1,0:T(8,128)(2,1)S(1)} %get-tuple-element.215), channel_id=1, source_target_pairs={{0,2},{1,3},{2,0},{3,1},{4,6},{5,7},{6,4},{7,5},{8,10},{9,11},{10,... | collective-permute-start | bytes 479240 | tf_op jit(solution)/shard_map/ppermute | solution.py:841
  13.0 15.8 %collective-permute-start.1 = (bf16[208,384]{1,0:T(8,128)(2,1)S(1)}, bf16[208,384]{1,0:T(8,128)(2,1)S(1)}, u32[]{:S(2)}, u32[]{:S(2)}) collective-permute-start(bf16[208,384]{1,0:T(8,128)(2,1)S(1)} %get-tuple-element.215), channel_id=1, source_target_pairs={{0,4},{1,5},{2,6},{3,7},{4,0},{5,1},{6,2},{7,3},{8,12},{9,13},{10,... | collective-permute-start | bytes 479240 | tf_op jit(solution)/shard_map/ppermute | solution.py:841
  15.5 13.3 %collective-permute-start.2 = (bf16[208,384]{1,0:T(8,128)(2,1)S(1)}, bf16[208,384]{1,0:T(8,128)(2,1)S(1)}, u32[]{:S(2)}, u32[]{:S(2)}) collective-permute-start(bf16[208,384]{1,0:T(8,128)(2,1)S(1)} %get-tuple-element.215), channel_id=1, source_target_pairs={{0,6},{1,7},{2,4},{3,5},{4,2},{5,3},{6,0},{7,1},{8,14},{9,15},{10,... | collective-permute-start | bytes 479240 | tf_op jit(solution)/shard_map/ppermute | solution.py:841
  28.9 13.8 %copy-start.5 = (f32[96,3072]{1,0:T(8,128)S(1)}, f32[96,3072]{1,0:T(8,128)}, u32[]{:S(2)}) copy-start(f32[96,3072]{1,0:T(8,128)} %param.29) | copy-start | bytes 3538948
  28.9 12.1 %collective-permute-start.3 = (bf16[4,208,384]{2,1,0:T(8,128)(2,1)S(1)}, bf16[4,208,384]{2,1,0:T(8,128)(2,1)S(1)}, u32[]{:S(2)}, u32[]{:S(2)}) collective-permute-start(bf16[4,208,384]{2,1,0:T(8,128)(2,1)S(1)} %pad_maximum_fusion), channel_id=1, source_target_pairs={{0,16},{1,17},{2,18},{3,19},{4,20},{5,21},{6,22},{7,23},{8,9},{9,8... | collective-permute-start | bytes 1916936 | tf_op jit(solution)/shard_map/ppermute | solution.py:845
  41.1 21.5 %copy-start.8 = (bf16[8,208,384]{2,1,0:T(8,128)(2,1)}, bf16[8,208,384]{2,1,0:T(8,128)(2,1)S(1)}, u32[]{:S(2)}) copy-start(bf16[8,208,384]{2,1,0:T(8,128)(2,1)S(1)} %constant_dynamic-update-slice_fusion.refs_5_) | copy-start | bytes 3833860
  41.1 21.2 %collective-permute-start.7 = (bf16[8,208,384]{2,1,0:T(8,128)(2,1)S(1)}, bf16[8,208,384]{2,1,0:T(8,128)(2,1)}, u32[]{:S(2)}, u32[]{:S(2)}) collective-permute-start(bf16[8,208,384]{2,1,0:T(8,128)(2,1)S(1)} %constant_dynamic-update-slice_fusion.refs_5_), channel_id=1, source_target_pairs={{0,1},{1,0},{2,3},{3,2},{4,5},{5,4},{6,7},{7,6},{8,24},{9,25},{10,... | collective-permute-start | bytes 3833864 | tf_op jit(solution)/shard_map/ppermute | solution.py:845
  42.7 19.7 %collective-permute-start.8 = (bf16[8,208,384]{2,1,0:T(8,128)(2,1)S(1)}, bf16[8,208,384]{2,1,0:T(8,128)(2,1)S(1)}, u32[]{:S(2)}, u32[]{:S(2)}) collective-permute-start(bf16[8,208,384]{2,1,0:T(8,128)(2,1)S(1)} %constant_dynamic-update-slice_fusion.refs_5_), channel_id=1, source_target_pairs={{0,8},{1,9},{2,10},{3,11},{4,12},{5,13},{6,14},{7,15},{8,0},{9,1},... | collective-permute-start | bytes 3833864 | tf_op jit(solution)/shard_map/ppermute | solution.py:833
  42.8 13.9 %collective-permute-start.4 = (bf16[48,1536]{1,0:T(8,128)(2,1)S(1)}, bf16[48,1536]{1,0:T(8,128)(2,1)S(1)}, u32[]{:S(2)}, u32[]{:S(2)}) collective-permute-start(bf16[48,1536]{1,0:T(8,128)(2,1)S(1)} %fusion.2), channel_id=1, source_target_pairs={{0,2},{1,3},{2,0},{3,1},{4,6},{5,7},{6,4},{7,5},{8,10},{9,11},{10,... | collective-permute-start | bytes 442376 | tf_op jit(solution)/shard_map/ppermute | solution.py:841
  45.3 11.9 %collective-permute-start.5 = (bf16[48,1536]{1,0:T(8,128)(2,1)S(1)}, bf16[48,1536]{1,0:T(8,128)(2,1)S(1)}, u32[]{:S(2)}, u32[]{:S(2)}) collective-permute-start(bf16[48,1536]{1,0:T(8,128)(2,1)S(1)} %fusion.2), channel_id=1, source_target_pairs={{0,4},{1,5},{2,6},{3,7},{4,0},{5,1},{6,2},{7,3},{8,12},{9,13},{10,... | collective-permute-start | bytes 442376 | tf_op jit(solution)/shard_map/ppermute | solution.py:841
  47.1 15.2 %collective-permute-start.6 = (bf16[48,1536]{1,0:T(8,128)(2,1)S(1)}, bf16[48,1536]{1,0:T(8,128)(2,1)S(1)}, u32[]{:S(2)}, u32[]{:S(2)}) collective-permute-start(bf16[48,1536]{1,0:T(8,128)(2,1)S(1)} %fusion.2), channel_id=1, source_target_pairs={{0,6},{1,7},{2,4},{3,5},{4,2},{5,3},{6,0},{7,1},{8,14},{9,15},{10,... | collective-permute-start | bytes 442376 | tf_op jit(solution)/shard_map/ppermute | solution.py:841
  62.2 5.2 %copy-start.3 = (s32[8]{0:T(128)S(1)}, s32[8]{0:T(128)}, u32[]{:S(2)}) copy-start(s32[8]{0:T(128)} %refs_1_.4) | copy-start | bytes 100
  62.3 5.2 %copy-start.4 = (s32[8]{0:T(128)S(1)}, s32[8]{0:T(128)}, u32[]{:S(2)}) copy-start(s32[8]{0:T(128)} %refs_2_.4) | copy-start | bytes 100
  62.4 3.4 %collective-permute-start.9 = (bf16[8,208,384]{2,1,0:T(8,128)(2,1)}, bf16[8,208,384]{2,1,0:T(8,128)(2,1)}, u32[]{:S(2)}, u32[]{:S(2)}) collective-permute-start(bf16[8,208,384]{2,1,0:T(8,128)(2,1)} %collective-permute-done.7.refs_6_), channel_id=1, source_target_pairs={{0,8},{1,9},{2,10},{3,11},{4,12},{5,13},{6,14},{7,15},{8,0},{9,1},... | collective-permute-start | bytes 3833864 | tf_op jit(solution)/shard_map/ppermute | solution.py:833
  63.5 22.5 %collective-permute-start.10 = (bf16[4,48,1536]{2,1,0:T(8,128)(2,1)S(1)}, bf16[4,48,1536]{2,1,0:T(8,128)(2,1)S(1)}, u32[]{:S(2)}, u32[]{:S(2)}) collective-permute-start(bf16[4,48,1536]{2,1,0:T(8,128)(2,1)S(1)} %pad_maximum_fusion.1.refs_9_), channel_id=1, source_target_pairs={{0,16},{1,17},{2,18},{3,19},{4,20},{5,21},{6,22},{7,23},{8,9},{9,8... | collective-permute-start | bytes 1769480 | tf_op jit(solution)/shard_map/ppermute | solution.py:845
  86.0 16.4 %copy-start = (bf16[8,48,1536]{2,1,0:T(8,128)(2,1)}, bf16[8,48,1536]{2,1,0:T(8,128)(2,1)S(1)}, u32[]{:S(2)}) copy-start(bf16[8,48,1536]{2,1,0:T(8,128)(2,1)S(1)} %constant_dynamic-update-slice_fusion.5.refs_4_.refs_8_) | copy-start | bytes 3538948
  86.0 16.7 %collective-permute-start.11 = (bf16[8,48,1536]{2,1,0:T(8,128)(2,1)S(1)}, bf16[8,48,1536]{2,1,0:T(8,128)(2,1)}, u32[]{:S(2)}, u32[]{:S(2)}) collective-permute-start(bf16[8,48,1536]{2,1,0:T(8,128)(2,1)S(1)} %constant_dynamic-update-slice_fusion.5.refs_4_.refs_8_), channel_id=1, source_target_pairs={{0,1},{1,0},{2,3},{3,2},{4,5},{5,4},{6,7},{7,6},{8,24},{9,25},{10,... | collective-permute-start | bytes 3538952 | tf_op jit(solution)/shard_map/ppermute | solution.py:845
  102.4 2.9 %collective-permute-start.12 = (bf16[8,48,1536]{2,1,0:T(8,128)(2,1)S(1)}, bf16[8,48,1536]{2,1,0:T(8,128)(2,1)S(1)}, u32[]{:S(2)}, u32[]{:S(2)}) collective-permute-start(bf16[8,48,1536]{2,1,0:T(8,128)(2,1)S(1)} %constant_dynamic-update-slice_fusion.5.refs_4_.refs_8_), channel_id=1, source_target_pairs={{0,8},{1,9},{2,10},{3,11},{4,12},{5,13},{6,14},{7,15},{8,0},{9,1},... | collective-permute-start | bytes 3538952 | tf_op jit(solution)/shard_map/ppermute | solution.py:833
  102.8 4.5 %collective-permute-start.13 = (bf16[8,48,1536]{2,1,0:T(8,128)(2,1)}, bf16[8,48,1536]{2,1,0:T(8,128)(2,1)S(1)}, u32[]{:S(2)}, u32[]{:S(2)}) collective-permute-start(bf16[8,48,1536]{2,1,0:T(8,128)(2,1)} %collective-permute-done.11.refs_9_), channel_id=1, source_target_pairs={{0,8},{1,9},{2,10},{3,11},{4,12},{5,13},{6,14},{7,15},{8,0},{9,1},... | collective-permute-start | bytes 3538952 | tf_op jit(solution)/shard_map/ppermute | solution.py:833
  127.8 5.7 %collective-permute-start.14 = (bf16[16,192,384]{2,1,0:T(8,128)(2,1)}, bf16[16,192,384]{2,1,0:T(8,128)(2,1)S(1)}, u32[]{:S(2)}, u32[]{:S(2)}) collective-permute-start(bf16[16,192,384]{2,1,0:T(8,128)(2,1)} %get-tuple-element.129), channel_id=1, source_target_pairs={{0,8},{1,9},{2,10},{3,11},{4,12},{5,13},{6,14},{7,15},{8,0},{9,1},... | collective-permute-start | bytes 7077896 | tf_op jit(solution)/shard_map/ppermute | solution.py:833
  134.0 16.5 %collective-permute-start.15 = (bf16[1536,384]{1,0:T(8,128)(2,1)S(1)}, bf16[1536,384]{1,0:T(8,128)(2,1)S(1)}, u32[]{:S(2)}, u32[]{:S(2)}) collective-permute-start(bf16[1536,384]{1,0:T(8,128)(2,1)S(1)} %get-tuple-element.139), channel_id=1, source_target_pairs={{0,1},{1,0},{2,3},{3,2},{4,5},{5,4},{6,7},{7,6},{8,24},{9,25},{10,... | collective-permute-start | bytes 3538952 | tf_op jit(solution)/shard_map/ppermute | solution.py:845
  150.9 10.6 %collective-permute-start.17 = (bf16[16,192,384]{2,1,0:T(8,128)(2,1)S(1)}, bf16[16,192,384]{2,1,0:T(8,128)(2,1)S(1)}, u32[]{:S(2)}, u32[]{:S(2)}) collective-permute-start(bf16[16,192,384]{2,1,0:T(8,128)(2,1)S(1)} %copy-done.19), channel_id=1, source_target_pairs={{0,8},{1,9},{2,10},{3,11},{4,12},{5,13},{6,14},{7,15},{8,0},{9,1},... | collective-permute-start | bytes 7077896 | tf_op jit(solution)/shard_map/ppermute | solution.py:833
  150.9 11.8 %collective-permute-start.16 = (bf16[768,384]{1,0:T(8,128)(2,1)S(1)}, bf16[768,384]{1,0:T(8,128)(2,1)S(1)}, u32[]{:S(2)}, u32[]{:S(2)}) collective-permute-start(bf16[768,384]{1,0:T(8,128)(2,1)S(1)} %get-tuple-element.147), channel_id=1, source_target_pairs={{0,16},{1,17},{2,18},{3,19},{4,20},{5,21},{6,22},{7,23},{8,9},{9,8... | collective-permute-start | bytes 1769480 | tf_op jit(solution)/shard_map/ppermute | solution.py:845
  162.0 19.2 %collective-permute-start.18 = (bf16[1536,384]{1,0:T(8,128)(2,1)S(1)}, bf16[1536,384]{1,0:T(8,128)(2,1)S(1)}, u32[]{:S(2)}, u32[]{:S(2)}) collective-permute-start(bf16[1536,384]{1,0:T(8,128)(2,1)S(1)} %get-tuple-element.159), channel_id=1, source_target_pairs={{0,1},{1,0},{2,3},{3,2},{4,5},{5,4},{6,7},{7,6},{8,24},{9,25},{10,... | collective-permute-start | bytes 3538952 | tf_op jit(solution)/shard_map/ppermute | solution.py:845
  162.9 20.7 %collective-permute-start.19 = (bf16[192,384]{1,0:T(8,128)(2,1)S(1)}, bf16[192,384]{1,0:T(8,128)(2,1)S(1)}, u32[]{:S(2)}, u32[]{:S(2)}) collective-permute-start(bf16[192,384]{1,0:T(8,128)(2,1)S(1)} %get-tuple-element.164), channel_id=1, source_target_pairs={{0,2},{1,3},{2,0},{3,1},{4,6},{5,7},{6,4},{7,5},{8,10},{9,11},{10,... | collective-permute-start | bytes 442376 | tf_op jit(solution)/shard_map/ppermute | solution.py:841
  164.8 18.8 %collective-permute-start.20 = (bf16[192,384]{1,0:T(8,128)(2,1)S(1)}, bf16[192,384]{1,0:T(8,128)(2,1)S(1)}, u32[]{:S(2)}, u32[]{:S(2)}) collective-permute-start(bf16[192,384]{1,0:T(8,128)(2,1)S(1)} %get-tuple-element.165), channel_id=1, source_target_pairs={{0,4},{1,5},{2,6},{3,7},{4,0},{5,1},{6,2},{7,3},{8,12},{9,13},{10,... | collective-permute-start | bytes 442376 | tf_op jit(solution)/shard_map/ppermute | solution.py:841
  165.5 18.2 %collective-permute-start.21 = (bf16[192,384]{1,0:T(8,128)(2,1)S(1)}, bf16[192,384]{1,0:T(8,128)(2,1)S(1)}, u32[]{:S(2)}, u32[]{:S(2)}) collective-permute-start(bf16[192,384]{1,0:T(8,128)(2,1)S(1)} %get-tuple-element.166), channel_id=1, source_target_pairs={{0,6},{1,7},{2,4},{3,5},{4,2},{5,3},{6,0},{7,1},{8,14},{9,15},{10,... | collective-permute-start | bytes 442376 | tf_op jit(solution)/shard_map/ppermute | solution.py:841
  167.4 13.1 %copy-start.1 = (f32[3,32,16]{2,1,0:T(8,128)S(1)}, f32[3,32,16]{2,1,0:T(8,128)}, u32[]{:S(2)}) copy-start(f32[3,32,16]{2,1,0:T(8,128)} %constant.117.clone.refs_1_) | copy-start | bytes 18436
  167.4 13.1 %copy-start.2 = (f32[3,32,8]{2,1,0:T(8,128)S(1)}, f32[3,32,8]{2,1,0:T(8,128)}, u32[]{:S(2)}) copy-start(f32[3,32,8]{2,1,0:T(8,128)} %constant.118.clone.refs_2_) | copy-start | bytes 9220
  181.2 14.4 %collective-permute-start.22 = (bf16[16,384]{1,0:T(8,128)(2,1)S(1)}, bf16[16,384]{1,0:T(8,128)(2,1)S(1)}, u32[]{:S(2)}, u32[]{:S(2)}) collective-permute-start(bf16[16,384]{1,0:T(8,128)(2,1)S(1)} %get-tuple-element.163.refs_6_), channel_id=1, source_target_pairs={{0,8},{1,9},{2,10},{3,11},{4,12},{5,13},{6,14},{7,15},{8,0},{9,1},... | collective-permute-start | bytes 36872 | tf_op jit(solution)/shard_map/ppermute | solution.py:833
  181.6 14.0 %collective-permute-start.23 = (bf16[768,384]{1,0:T(8,128)(2,1)S(1)}, bf16[768,384]{1,0:T(8,128)(2,1)S(1)}, u32[]{:S(2)}, u32[]{:S(2)}) collective-permute-start(bf16[768,384]{1,0:T(8,128)(2,1)S(1)} %get-tuple-element.169), channel_id=1, source_target_pairs={{0,16},{1,17},{2,18},{3,19},{4,20},{5,21},{6,22},{7,23},{8,9},{9,8... | collective-permute-start | bytes 1769480 | tf_op jit(solution)/shard_map/ppermute | solution.py:845
  183.7 12.2 %copy-start.11 = (pred[16]{0:T(512)(128)(4,1)S(1)}, pred[16]{0:T(512)(128)(4,1)}, u32[]{:S(2)}) copy-start(pred[16]{0:T(512)(128)(4,1)} %constant.116.clone.1) | copy-start | bytes 52
  195.6 4.8 %collective-permute-start.24 = (bf16[16,192,384]{2,1,0:T(8,128)(2,1)}, bf16[16,192,384]{2,1,0:T(8,128)(2,1)S(1)}, u32[]{:S(2)}, u32[]{:S(2)}) collective-permute-start(bf16[16,192,384]{2,1,0:T(8,128)(2,1)} %get-tuple-element.172), channel_id=1, source_target_pairs={{0,8},{1,9},{2,10},{3,11},{4,12},{5,13},{6,14},{7,15},{8,0},{9,1},... | collective-permute-start | bytes 7077896 | tf_op jit(solution)/shard_map/ppermute | solution.py:833
  195.9 21.1 %collective-permute-start.27 = (bf16[192,384]{1,0:T(8,128)(2,1)S(1)}, bf16[192,384]{1,0:T(8,128)(2,1)S(1)}, u32[]{:S(2)}, u32[]{:S(2)}) collective-permute-start(bf16[192,384]{1,0:T(8,128)(2,1)S(1)} %get-tuple-element.182), channel_id=1, source_target_pairs={{0,2},{1,3},{2,0},{3,1},{4,6},{5,7},{6,4},{7,5},{8,10},{9,11},{10,... | collective-permute-start | bytes 442376 | tf_op jit(solution)/shard_map/ppermute | solution.py:841
  196.1 20.9 %collective-permute-start.28 = (bf16[192,384]{1,0:T(8,128)(2,1)S(1)}, bf16[192,384]{1,0:T(8,128)(2,1)S(1)}, u32[]{:S(2)}, u32[]{:S(2)}) collective-permute-start(bf16[192,384]{1,0:T(8,128)(2,1)S(1)} %get-tuple-element.183), channel_id=1, source_target_pairs={{0,4},{1,5},{2,6},{3,7},{4,0},{5,1},{6,2},{7,3},{8,12},{9,13},{10,... | collective-permute-start | bytes 442376 | tf_op jit(solution)/shard_map/ppermute | solution.py:841
  197.9 19.1 %collective-permute-start.29 = (bf16[192,384]{1,0:T(8,128)(2,1)S(1)}, bf16[192,384]{1,0:T(8,128)(2,1)S(1)}, u32[]{:S(2)}, u32[]{:S(2)}) collective-permute-start(bf16[192,384]{1,0:T(8,128)(2,1)S(1)} %get-tuple-element.184), channel_id=1, source_target_pairs={{0,6},{1,7},{2,4},{3,5},{4,2},{5,3},{6,0},{7,1},{8,14},{9,15},{10,... | collective-permute-start | bytes 442376 | tf_op jit(solution)/shard_map/ppermute | solution.py:841
  201.1 6.8 %collective-permute-start.26 = (bf16[192,384]{1,0:T(8,128)(2,1)S(1)}, bf16[192,384]{1,0:T(8,128)(2,1)S(1)}, u32[]{:S(2)}, u32[]{:S(2)}) collective-permute-start(bf16[192,384]{1,0:T(8,128)(2,1)S(1)} %total.3.refs_4_), channel_id=1, source_target_pairs={{0,16},{1,17},{2,18},{3,19},{4,20},{5,21},{6,22},{7,23},{8,24},{9,... | collective-permute-start | bytes 442376 | tf_op jit(solution)/shard_map/ppermute | solution.py:837
  201.6 16.3 %collective-permute-start.25 = (bf16[1552,384]{1,0:T(8,128)(2,1)S(1)}, bf16[1552,384]{1,0:T(8,128)(2,1)S(1)}, u32[]{:S(2)}, u32[]{:S(2)}) collective-permute-start(bf16[1552,384]{1,0:T(8,128)(2,1)S(1)} %get-tuple-element.180), channel_id=1, source_target_pairs={{0,1},{1,0},{2,3},{3,2},{4,5},{5,4},{6,7},{7,6},{8,24},{9,25},{10,... | collective-permute-start | bytes 3575816 | tf_op jit(solution)/shard_map/ppermute | solution.py:845
  207.9 12.0 %collective-permute-start.33 = (bf16[48,3072]{1,0:T(8,128)(2,1)S(1)}, bf16[48,3072]{1,0:T(8,128)(2,1)S(1)}, u32[]{:S(2)}, u32[]{:S(2)}) collective-permute-start(bf16[48,3072]{1,0:T(8,128)(2,1)S(1)} %pad_maximum_fusion.4), channel_id=1, source_target_pairs={{0,8},{1,9},{2,10},{3,11},{4,12},{5,13},{6,14},{7,15},{8,0},{9,1},... | collective-permute-start | bytes 884744 | tf_op jit(solution)/shard_map/ppermute | solution.py:833
  218.3 6.1 %collective-permute-start.31 = (bf16[192,384]{1,0:T(8,128)(2,1)S(1)}, bf16[192,384]{1,0:T(8,128)(2,1)S(1)}, u32[]{:S(2)}, u32[]{:S(2)}) collective-permute-start(bf16[192,384]{1,0:T(8,128)(2,1)S(1)} %total.4), channel_id=1, source_target_pairs={{0,16},{1,17},{2,18},{3,19},{4,20},{5,21},{6,22},{7,23},{8,24},{9,... | collective-permute-start | bytes 442376 | tf_op jit(solution)/shard_map/ppermute | solution.py:837
  220.1 11.5 %collective-permute-start.30 = (bf16[784,384]{1,0:T(8,128)(2,1)S(1)}, bf16[784,384]{1,0:T(8,128)(2,1)S(1)}, u32[]{:S(2)}, u32[]{:S(2)}) collective-permute-start(bf16[784,384]{1,0:T(8,128)(2,1)S(1)} %get-tuple-element.186), channel_id=1, source_target_pairs={{0,16},{1,17},{2,18},{3,19},{4,20},{5,21},{6,22},{7,23},{8,9},{9,8... | collective-permute-start | bytes 1806344 | tf_op jit(solution)/shard_map/ppermute | solution.py:845
  224.5 12.1 %collective-permute-start.32 = (bf16[192,768]{1,0:T(8,128)(2,1)S(1)}, bf16[192,768]{1,0:T(8,128)(2,1)S(1)}, u32[]{:S(2)}, u32[]{:S(2)}) collective-permute-start(bf16[192,768]{1,0:T(8,128)(2,1)S(1)} %pad_maximum_fusion.3), channel_id=1, source_target_pairs={{0,8},{1,9},{2,10},{3,11},{4,12},{5,13},{6,14},{7,15},{8,0},{9,1},... | collective-permute-start | bytes 884744 | tf_op jit(solution)/shard_map/ppermute | solution.py:833
  232.2 7.8 %collective-permute-start.34 = (bf16[208,384]{1,0:T(8,128)(2,1)S(1)}, bf16[208,384]{1,0:T(8,128)(2,1)S(1)}, u32[]{:S(2)}, u32[]{:S(2)}) collective-permute-start(bf16[208,384]{1,0:T(8,128)(2,1)S(1)} %get-tuple-element.191), channel_id=1, source_target_pairs={{0,2},{1,3},{2,0},{3,1},{4,6},{5,7},{6,4},{7,5},{8,10},{9,11},{10,... | collective-permute-start | bytes 479240 | tf_op jit(solution)/shard_map/ppermute | solution.py:841
  232.7 13.1 %collective-permute-start.35 = (bf16[208,384]{1,0:T(8,128)(2,1)S(1)}, bf16[208,384]{1,0:T(8,128)(2,1)S(1)}, u32[]{:S(2)}, u32[]{:S(2)}) collective-permute-start(bf16[208,384]{1,0:T(8,128)(2,1)S(1)} %get-tuple-element.192), channel_id=1, source_target_pairs={{0,4},{1,5},{2,6},{3,7},{4,0},{5,1},{6,2},{7,3},{8,12},{9,13},{10,... | collective-permute-start | bytes 479240 | tf_op jit(solution)/shard_map/ppermute | solution.py:841
  234.4 11.5 %collective-permute-start.36 = (bf16[208,384]{1,0:T(8,128)(2,1)S(1)}, bf16[208,384]{1,0:T(8,128)(2,1)S(1)}, u32[]{:S(2)}, u32[]{:S(2)}) collective-permute-start(bf16[208,384]{1,0:T(8,128)(2,1)S(1)} %get-tuple-element.193), channel_id=1, source_target_pairs={{0,6},{1,7},{2,4},{3,5},{4,2},{5,3},{6,0},{7,1},{8,14},{9,15},{10,... | collective-permute-start | bytes 479240 | tf_op jit(solution)/shard_map/ppermute | solution.py:841
  245.9 5.3 %collective-permute-start.37 = (bf16[208,384]{1,0:T(8,128)(2,1)S(1)}, bf16[208,384]{1,0:T(8,128)(2,1)S(1)}, u32[]{:S(2)}, u32[]{:S(2)}) collective-permute-start(bf16[208,384]{1,0:T(8,128)(2,1)S(1)} %total.5), channel_id=1, source_target_pairs={{0,16},{1,17},{2,18},{3,19},{4,20},{5,21},{6,22},{7,23},{8,24},{9,... | collective-permute-start | bytes 479240 | tf_op jit(solution)/shard_map/ppermute | solution.py:837
  251.4 1.7 collective-permute-start.38
  (13 other events, 31.0 us)
Sparse Core Ops, SparseCore 0:
  11.6 78.3 all-gather.2
where the time goes:
time: 266 us; the launch traced here: 264 us
  Pallas kernels  116 us (44%)
  waiting for transfers between devices  76.4 us (29%)
  starting transfers between devices  45.6 us (17%)
  between operations  15 us (6%)
  other arithmetic  5.5 us (2%)
  local copies, waits for them, and re-layouts  4.86 us (2%)
    pallas_call x23, Pallas kernels, kernel_call(): return call(*args, *deps)  116 us
    ppermute x15, waiting for transfers between devices, to_z(): return lax.ppermute(v, AXES, route(lambda x, c, z, y: (x, c, z ^ k, y)))  35.1 us
    ppermute x15, starting transfers between devices, to_z(): return lax.ppermute(v, AXES, route(lambda x, c, z, y: (x, c, z ^ k, y)))  24.6 us
    ppermute x10, waiting for transfers between devices, to_cross(): lax.ppermute(v, AXES, route(lambda x, c, z, y: (1 - x, c, z, y) if c == f...  19.8 us
    ppermute x10, starting transfers between devices, to_cross(): lax.ppermute(v, AXES, route(lambda x, c, z, y: (1 - x, c, z, y) if c == f...  14.5 us
    ppermute x3, waiting for transfers between devices, to_x(): return lax.ppermute(v, AXES, route(lambda x, c, z, y: (1 - x, c, z, y)))  12.3 us
    ppermute x11, waiting for transfers between devices, to_core(): return lax.ppermute(v, AXES, route(lambda x, c, z, y: (x, 1 - c, z, y)))  6.13 us
  transfers between devices with their start and end apart: 40, of which 20 were waited for; matrix products, arithmetic and copies ran while one was open for 2% of the time, Pallas kernels for 35%

commit v1 on v0

--- a/solution.py
+++ b/solution.py
@@ -651,11 +651,18 @@
 
 
 def attention_back_kernel(seq, *refs):
-    mix_ref, joined_ref, probs_ref, grad_ref, sums_ref = refs
+    mix_ref, joined_ref, probs_ref, *others_far = refs[:6]
+    grad_ref, sums_ref, near_ref, *others, sem = refs[6:]
+    step = pl.program_id(0)
+    ahead = [
+        pltpu.make_async_copy(source, target, sem.at[i])
+        for i, (source, target) in enumerate(zip(others_far, others))
+    ]
     d = mix_ref.shape[1]
 
-    @pl.when(pl.program_id(0) == 0)
+    @pl.when(step == 0)
     def _():
+        go(ahead)
         sums_ref[...] = jnp.zeros_like(sums_ref)
 
     for p in range(mix_ref.shape[0] // seq):
@@ -675,11 +682,17 @@
             grad_ref[here, two] = nn(scores, split_heads(joined_ref[here, one])).astype(BF)
             keys = split_heads(joined_ref[here, two])
             grad_ref[here, one] = (nn(turn_heads(scores), keys) * 0.125).astype(BF)
+    tile = mix_ref.shape[0]
+    near_ref[pl.ds(pl.multiple_of(step * tile, tile), tile), :] = grad_ref[...]
     sums_ref[0:1, :] += jnp.sum(grad_ref[:, :d].astype(F32), axis=0, keepdims=True)
     sums_ref[1:2, :] += jnp.sum(grad_ref[:, 2 * d :].astype(F32), axis=0, keepdims=True)
 
-
-def attention_back(mix, joined, probs, seq, deps=()):
+    @pl.when(step == pl.num_programs(0) - 1)
+    def _():
+        done(ahead)
+
+
+def attention_back(mix, joined, probs, others, seq, deps=()):
     n, d = mix.shape
     tile = 2 * seq
     return kernel_call(
@@ -689,14 +702,20 @@
             rows((tile, d)),
             rows((tile, 3 * d)),
             rows((2, d // 128, seq, 2 * seq)),
+            ANY,
+            ANY,
+            ANY,
         ],
-        [near(mix), far(joined), far(probs)],
+        [near(mix), far(joined), far(probs), *map(far, others)],
         grid=(n // tile,),
-        out_specs=[rows((tile, 3 * d)), fixed((8, d))],
+        out_specs=[rows((tile, 3 * d)), fixed((8, d))] + [WHOLE] * 4,
         out_shape=[
             HBM((n, 3 * d), BF),
             jax.ShapeDtypeStruct((8, d), F32),
-        ],
+            VMEM((n, 3 * d), BF),
+        ]
+        + [VMEM((n, d), BF)] * 3,
+        scratch_shapes=[pltpu.SemaphoreType.DMA((3,))],
         cost_estimate=pl.CostEstimate(
             flops=16 * n * d * d, bytes_accessed=30 * n * d, transcendentals=0
         ),
@@ -706,30 +725,15 @@
 
 
 def qkv_grad_kernel(fast, *refs):
-    meta, grad_far, x_far, low_far, mix_far = refs[:5]
+    meta, grad_ref, x_ref, low_ref, mix_ref = refs[:5]
     outs = refs[5:7]
-    token_ref, whole, whole_out, grad_ref, x_ref, low_ref, mix_ref, sem_a, sem_b, sem_c = refs[7:]
+    token_ref, whole, whole_out, sem_a, sem_b = refs[7:]
+    token_ref[...] = jnp.zeros_like(token_ref)
     total, d = whole.shape
-    width = total // 6
-    columns = [pl.ds(i * width, width) for i in range(6)]
-    reads = [
-        pltpu.make_async_copy(x_far, x_ref, sem_c.at[0]),
-        pltpu.make_async_copy(low_far, low_ref, sem_c.at[1]),
-        pltpu.make_async_copy(mix_far, mix_ref, sem_c.at[2]),
-    ]
-    grads = [
-        pltpu.make_async_copy(grad_far.at[:, here], grad_ref.at[:, here], sem_c.at[3 + i])
-        for i, here in enumerate(columns)
-    ]
-    go(reads[:1] + grads + reads[1:])
-    token_ref[...] = jnp.zeros_like(token_ref)
     waits = []
-    done(reads[:1])
     for i in range(2):
-        for k in range(3 * i, 3 * i + 3):
-            done([grads[k]])
-            here = slice(k * width, (k + 1) * width)
-            whole[here, :] = tn(grad_ref[:, here], x_ref[...]).astype(BF)
+        here = slice(i * total // 2, (i + 1) * total // 2)
+        whole[here, :] = tn(grad_ref[:, here], x_ref[...]).astype(BF)
         if fast:
             go(
                 tile_copies(
@@ -738,7 +742,6 @@
                 )
             )
             waits += tile_waits(whole, outs, sem_a.at[i], 8, 0, total // 16, d // 2)
-    done(reads[1:])
     whole_out[...] = tn(low_ref[...], mix_ref[...]).astype(BF)
     if fast:
         go(
@@ -766,20 +769,15 @@
     return kernel_call(
         functools.partial(qkv_grad_kernel, fast),
         deps,
-        [SMEM, ANY, ANY, ANY, ANY],
-        [meta, far(grad), far(x), far(low), far(mix)],
+        [SMEM, WHOLE, WHOLE, WHOLE, WHOLE],
+        [meta, near(grad), near(x), near(low), near(mix)],
         out_specs=([WHOLE, ANY] if fast else [ANY] * 2) + [WHOLE],
         out_shape=shapes + [TOKEN],
         scratch_shapes=[
             pltpu.VMEM((3 * d, d), BF),
             pltpu.VMEM((d, d), BF),
-            pltpu.VMEM((n, 3 * d), BF),
-            pltpu.VMEM((n, d), BF),
-            pltpu.VMEM((n, d), BF),
-            pltpu.VMEM((n, d), BF),
             pltpu.SemaphoreType.DMA((2, 16)),
             pltpu.SemaphoreType.DMA((32,)),
-            pltpu.SemaphoreType.DMA((9,)),
         ],
         cost_estimate=pl.CostEstimate(
             flops=16 * n * d * d, bytes_accessed=16 * n * d, transcendentals=0
@@ -1245,7 +1243,9 @@
         deps = [down_sum.add_last([sums_first]), up_sum.add_core([sums_first])]
         down_sum.along()
         up_sum.cross(1)
-    grad_joined, sums_attn = attention_back(grad_mix, joined, probs, seq, deps)
+    grad_joined, sums_attn, joined_near, *others = attention_back(
+        grad_mix, joined, probs, [flat, attn_low, mix], seq, deps
+    )
     grad_vectors = [
         jnp.concatenate([sums_attn[0:1], sums_attn[1:2]], axis=1),
         sums_first[2:3],
@@ -1262,7 +1262,7 @@
         deps = [up_sum.add_cross([sums_attn]), small_low] + down_sum.got
         up_sum.cross(0)
         small_got = to_core(small_low)
-    qkv_out = qkv_grad(fast, meta, grad_joined, flat, attn_low, mix, deps)
+    qkv_out = qkv_grad(fast, meta, joined_near, *others, deps)
     qkv_grads, token = qkv_out[:2], qkv_out[2]
     if fast:
         small_got, up_sum.got = after((small_got, up_sum.got), token)

time: 266 us -> 264 us (level)
  Pallas kernels: 116 us -> 112 us
  waiting for transfers between devices: 76.4 us -> 80 us
    pallas_call x23, Pallas kernels: 116 us -> 112 us  [kernel_call(): return call(*args, *deps)]
  transfers between devices with their start and end apart: 40 -> 40, of which waited for: 20 -> 20; matrix products, arithmetic and copies ran while one was open for 2% -> 2% of each run, Pallas kernels for 35% -> 34%
where the time goes in v1:
time: 264 us; the launch traced here: 262 us
  Pallas kernels  112 us (42%)
  waiting for transfers between devices  80 us (30%)
  starting transfers between devices  43.4 us (16%)
  between operations  15 us (6%)
  other arithmetic  5.5 us (2%)
  local copies, waits for them, and re-layouts  4.86 us (2%)
    pallas_call x23, Pallas kernels, kernel_call(): return call(*args, *deps)  112 us
    ppermute x15, waiting for transfers between devices, to_z(): return lax.ppermute(v, AXES, route(lambda x, c, z, y: (x, c, z ^ k, y)))  35.5 us
    ppermute x15, starting transfers between devices, to_z(): return lax.ppermute(v, AXES, route(lambda x, c, z, y: (x, c, z ^ k, y)))  24.6 us
    ppermute x10, waiting for transfers between devices, to_cross(): lax.ppermute(v, AXES, route(lambda x, c, z, y: (1 - x, c, z, y) if c == f...  22.2 us
    ppermute x10, starting transfers between devices, to_cross(): lax.ppermute(v, AXES, route(lambda x, c, z, y: (1 - x, c, z, y) if c == f...  14.5 us
    ppermute x3, waiting for transfers between devices, to_x(): return lax.ppermute(v, AXES, route(lambda x, c, z, y: (1 - x, c, z, y)))  13.1 us
    ppermute x11, waiting for transfers between devices, to_core(): return lax.ppermute(v, AXES, route(lambda x, c, z, y: (x, 1 - c, z, y)))  6.13 us
  transfers between devices with their start and end apart: 40, of which 20 were waited for; matrix products, arithmetic and copies ran while one was open for 2% of the time, Pallas kernels for 34%

profile of v1, /device:TPU:0, one launch (start us, length us, event | category | flops | bytes accessed | tf_op | source)
XLA Modules:
  0.0 261.5 jit_solution(11327727168038996341)
XLA Ops:
  7.4 1.4 slice_select_fusion
  9.9 3.1 %collective-permute-start = (bf16[208,384]{1,0:T(8,128)(2,1)S(1)}, bf16[208,384]{1,0:T(8,128)(2,1)S(1)}, u32[]{:S(2)}, u32[]{:S(2)}) collective-permute-start(bf16[208,384]{1,0:T(8,128)(2,1)S(1)} %get-tuple-element.223), channel_id=1, source_target_pairs={{0,2},{1,3},{2,0},{3,1},{4,6},{5,7},{6,4},{7,5},{8,10},{9,11},{10,... | collective-permute-start | bytes 479240 | tf_op jit(solution)/shard_map/ppermute | solution.py:839
  13.0 2.6 collective-permute-start.1
  15.6 3.9 %collective-permute-done = bf16[208,384]{1,0:T(8,128)(2,1)S(1)} collective-permute-done((bf16[208,384]{1,0:T(8,128)(2,1)S(1)}, bf16[208,384]{1,0:T(8,128)(2,1)S(1)}, u32[]{:S(2)}, u32[]{:S(2)}) %collective-permute-start) | collective-permute-done | bytes 159776 | tf_op jit(solution)/shard_map/ppermute | solution.py:839
  19.4 9.4 %collective-permute-done.1 = bf16[208,384]{1,0:T(8,128)(2,1)S(1)} collective-permute-done((bf16[208,384]{1,0:T(8,128)(2,1)S(1)}, bf16[208,384]{1,0:T(8,128)(2,1)S(1)}, u32[]{:S(2)}, u32[]{:S(2)}) %collective-permute-start.1) | collective-permute-done | bytes 159776 | tf_op jit(solution)/shard_map/ppermute | solution.py:839
  28.9 1.6 collective-permute-start.3
  30.6 10.4 %collective-permute-done.3 = bf16[4,208,384]{2,1,0:T(8,128)(2,1)S(1)} collective-permute-done((bf16[4,208,384]{2,1,0:T(8,128)(2,1)S(1)}, bf16[4,208,384]{2,1,0:T(8,128)(2,1)S(1)}, u32[]{:S(2)}, u32[]{:S(2)}) %collective-permute-start.3) | collective-permute-done | bytes 639008 | tf_op jit(solution)/shard_map/ppermute | solution.py:843
  41.1 1.6 collective-permute-start.7
  42.8 2.5 collective-permute-start.4
  45.3 1.8 collective-permute-start.5
  47.1 1.4 collective-permute-start.6
  48.5 8.2 %collective-permute-done.4 = bf16[48,1536]{1,0:T(8,128)(2,1)S(1)} collective-permute-done((bf16[48,1536]{1,0:T(8,128)(2,1)S(1)}, bf16[48,1536]{1,0:T(8,128)(2,1)S(1)}, u32[]{:S(2)}, u32[]{:S(2)}) %collective-permute-start.4) | collective-permute-done | bytes 147488 | tf_op jit(solution)/shard_map/ppermute | solution.py:839
  57.2 5.0 %collective-permute-done.6 = bf16[48,1536]{1,0:T(8,128)(2,1)S(1)} collective-permute-done((bf16[48,1536]{1,0:T(8,128)(2,1)S(1)}, bf16[48,1536]{1,0:T(8,128)(2,1)S(1)}, u32[]{:S(2)}, u32[]{:S(2)}) %collective-permute-start.6) | collective-permute-done | bytes 147488 | tf_op jit(solution)/shard_map/ppermute | solution.py:839
  63.5 2.0 collective-permute-start.10
  67.5 18.5 %attention_forward.1 = (bf16[1024,2304]{1,0:T(8,128)(2,1)}, bf16[8,6,128,256]{3,2,1,0:T(8,128)(2,1)}, bf16[1024,768]{1,0:T(8,128)(2,1)}, bf16[1024,768]{1,0:T(8,...) custom-call(s32[4]{0:T(128)S(1)} %pad_add_fusion.refs_0_, ...), custom_call_target="tpu_custom_call" | custom-call | flops 4831838208 | bytes 12582912 | tf_op jit(solution)/shard_map/attention_forward/pallas_call | solution.py:62
  86.9 3.0 %all-gather.3.cloned.1.call-done = bf16[6144,384]{1,0:T(8,128)(2,1)} async-done(((bf16[192,384]{1,0:T(8,128)(2,1)}), bf16[6144,384]{1,0:T(8,128)(2,1)}) %all-gather.3.cloned.1.call-update) | async-done | bytes 4718608 | tf_op jit(solution)/shard_map/all_gather | solution.py:1171
  90.0 12.4 %up_forward.1 = (bf16[1024,3072]{1,0:T(8,128)(2,1)S(1)}, bf16[1024,3072]{1,0:T(8,128)(2,1)S(1)}, f32[8,128]{1,0:T(8,128)}) custom-call(s32[4]{0:T(128)S(1)} %pad_add_fusion.refs_0_, bf16[1024,768]{1,0:T(8,128)(2,1)} %get-tuple-element.116.refs_1_.refs_2_, f32[1,3072]{1,0:T(1,128)S(1)} %bitcast.37, bf16[32,192,384]{2,1,0:T(8,128)(2,1)} %bitcast.48, ...), custom_call_target="tpu_custom_call" | custom-call | flops 9663676416 | bytes 12582912 | tf_op jit(solution)/shard_map/up_forward/pallas_call | solution.py:62
  103.0 2.3 collective-permute-done.12.refs_10_
  105.3 1.9 collective-permute-done.13.refs_11_
  107.2 20.5 %down_forward.1 = (bf16[1024,768]{1,0:T(8,128)(2,1)}, f32[1024,768]{1,0:T(8,128)}, bf16[1024,768]{1,0:T(8,128)(2,1)S(1)}, f32[8,768]{1,0:T(8,128)S(1)}, bf16[768...) custom-call(s32[4]{0:T(128)S(1)} %pad_add_fusion.refs_0_, ...), custom_call_target="tpu_custom_call", output_to_operand_aliasing={{5}: (4, {})} | custom-call | flops 28991029248 | bytes 6291456 | tf_op jit(solution)/shard_map/down_forward/pallas_call | solution.py:62
  128.1 5.4 %hidden_grad.1 = (bf16[1024,3072]{1,0:T(8,128)(2,1)S(1)}, f32[1,3072]{1,0:T(1,128)S(1)}) custom-call(bf16[1024,768]{1,0:T(8,128)(2,1)S(1)} %get-tuple-element.126.refs_0_, bf16[1024,3072]{1,0:T(8,128)(2,1)S(1)} %get-tuple-element.127.refs_1_, bf16[768,3072]{1,0:T(8,128)(2,1)S(1)} %get-tuple-element.128.refs_2_), custom_call_target="tpu_custom_call" | custom-call | flops 9663676416 | bytes 12582912 | tf_op jit(solution)/shard_map/hidden_grad/pallas_call | solution.py:62
  134.0 2.3 collective-permute-start.15
  136.4 10.0 %up_grad.1 = (bf16[16,192,384]{2,1,0:T(8,128)(2,1)S(1)}, bf16[16,192,384]{2,1,0:T(8,128)(2,1)}, f32[8,128]{1,0:T(8,128)S(1)}, bf16[1024,3072]{1,0:T(8,128)(2,1)S...) custom-call(s32[4]{0:T(128)S(1)} %pad_add_fusion.refs_0_, ...), custom_call_target="tpu_custom_call", output_to_operand_aliasing={{3}: (1, {})} | custom-call | flops 9663676416 | bytes 6291456 | tf_op jit(solution)/shard_map/up_grad/pallas_call | solution.py:62
  146.4 4.2 %collective-permute-done.15.refs_1_ = bf16[1536,384]{1,0:T(8,128)(2,1)S(1)} collective-permute-done((bf16[1536,384]{1,0:T(8,128)(2,1)S(1)}, bf16[1536,384]{1,0:T(8,128)(2,1)S(1)}, u32[]{:S(2)}, u32[]{:S(2)}) %collective-permute-start.15) | collective-permute-done | bytes 1179680 | tf_op jit(solution)/shard_map/ppermute | solution.py:843
  150.9 1.5 collective-permute-start.16
  152.5 9.0 %first_back.1 = (f32[1024,768]{1,0:T(8,128)}, bf16[1024,768]{1,0:T(8,128)(2,1)}, bf16[1024,768]{1,0:T(8,128)(2,1)S(1)}, f32[8,768]{1,0:T(8,128)S(1)}) custom-call(f32[1024,768]{1,0:T(8,128)S(1)} %get-tuple-element.136.refs_0_, bf16[1024,3072]{1,0:T(8,128)(2,1)S(1)} %get-tuple-element.137.refs_1_, bf16[3072,768]{1,0:T(8,128)(2,1)S(1)} %get-tuple-element.138.refs_2_, ...), custom_call_target="tpu_custom_call" | custom-call | flops 9663676416 | bytes 6291456 | tf_op jit(solution)/shard_map/first_back/pallas_call | solution.py:62
  162.9 1.9 collective-permute-start.19
  165.5 1.9 collective-permute-start.21
  167.4 13.7 %attention_back.1 = (bf16[1024,2304]{1,0:T(8,128)(2,1)}, f32[8,768]{1,0:T(8,128)S(1)}, bf16[1024,2304]{1,0:T(8,128)(2,1)S(1)}, bf16[1024,768]{1,0:T(8,128)(2,1)S...) custom-call(bf16[1024,768]{1,0:T(8,128)(2,1)S(1)} %get-tuple-element.147.refs_0_, ...), custom_call_target="tpu_custom_call" | custom-call | flops 9663676416 | bytes 23592960 | tf_op jit(solution)/shard_map/attention_back/pallas_call | solution.py:62
  182.2 2.1 collective-permute-start.23
  184.3 7.8 %qkv_grad.1 = (bf16[16,192,384]{2,1,0:T(8,128)(2,1)S(1)}, bf16[16,192,384]{2,1,0:T(8,128)(2,1)}, f32[8,128]{1,0:T(8,128)}) custom-call(s32[4]{0:T(128)S(1)} %pad_add_fusion.refs_0_, bf16[1024,2304]{1,0:T(8,128)(2,1)S(1)} %get-tuple-element.162.refs_1_, bf16[1024,768]{1,0:T(8,128)(2,1)S(1)} %get-tuple-element.163.refs_2_, ...), custom_call_target="tpu_custom_call" | custom-call | flops 9663676416 | bytes 12582912 | tf_op jit(solution)/shard_map/qkv_grad/pallas_call | solution.py:62
  193.4 1.6 collective-permute-start.28
  194.9 2.0 collective-permute-start.29
  197.6 2.0 collective-permute-start.26
  199.8 4.5 %collective-permute-done.26.refs_4_ = bf16[192,384]{1,0:T(8,128)(2,1)S(1)} collective-permute-done((bf16[192,384]{1,0:T(8,128)(2,1)S(1)}, bf16[192,384]{1,0:T(8,128)(2,1)S(1)}, u32[]{:S(2)}, u32[]{:S(2)}) %collective-permute-start.26) | collective-permute-done | bytes 147488 | tf_op jit(solution)/shard_map/ppermute | solution.py:835
  204.5 9.0 %tokens_back.1 = (f32[1024,768]{1,0:T(8,128)}, f32[8,128]{1,0:T(8,128)S(1)}) custom-call(f32[1024,768]{1,0:T(8,128)} %get-tuple-element.146.refs_0_, bf16[1024,2304]{1,0:T(8,128)(2,1)} %get-tuple-element.160.refs_1_, bf16[2304,768]{1,0:T(8,128)(2,1)} %get-tuple-element.161.refs_2_, f32[8,128]{1,0:T(8,128)S(1)} %get-tuple-element.184.refs_4_.refs_3_, ...), custom_call_target="tpu_custom_call" | custom-call | flops 7247757312 | bytes 11010048 | tf_op jit(solution)/shard_map/tokens_back/pallas_call | solution.py:62
  213.5 2.4 collective-permute-done.25.refs_1_
  216.6 2.0 collective-permute-start.30
  218.6 4.0 %collective-permute-done.31.refs_3_ = bf16[192,384]{1,0:T(8,128)(2,1)S(1)} collective-permute-done((bf16[192,384]{1,0:T(8,128)(2,1)S(1)}, bf16[192,384]{1,0:T(8,128)(2,1)S(1)}, u32[]{:S(2)}, u32[]{:S(2)}) %collective-permute-start.31) | collective-permute-done | bytes 147488 | tf_op jit(solution)/shard_map/ppermute | solution.py:835
  222.8 1.1 maximum_convert_fusion.1
  223.9 5.2 %collective-permute-done.30.refs_1_ = bf16[784,384]{1,0:T(8,128)(2,1)S(1)} collective-permute-done((bf16[784,384]{1,0:T(8,128)(2,1)S(1)}, bf16[784,384]{1,0:T(8,128)(2,1)S(1)}, u32[]{:S(2)}, u32[]{:S(2)}) %collective-permute-start.30) | collective-permute-done | bytes 602144 | tf_op jit(solution)/shard_map/ppermute | solution.py:843
  229.7 2.2 collective-permute-start.35
  231.9 2.2 collective-permute-start.36
  235.3 1.4 collective-permute-done.34.refs_1_
  236.6 7.2 %collective-permute-done.35.refs_2_ = bf16[208,384]{1,0:T(8,128)(2,1)S(1)} collective-permute-done((bf16[208,384]{1,0:T(8,128)(2,1)S(1)}, bf16[208,384]{1,0:T(8,128)(2,1)S(1)}, u32[]{:S(2)}, u32[]{:S(2)}) %collective-permute-start.35) | collective-permute-done | bytes 159776 | tf_op jit(solution)/shard_map/ppermute | solution.py:839
  244.6 4.7 %collective-permute-done.37 = bf16[208,384]{1,0:T(8,128)(2,1)S(1)} collective-permute-done((bf16[208,384]{1,0:T(8,128)(2,1)S(1)}, bf16[208,384]{1,0:T(8,128)(2,1)S(1)}, u32[]{:S(2)}, u32[]{:S(2)}) %collective-permute-start.37) | collective-permute-done | bytes 159776 | tf_op jit(solution)/shard_map/ppermute | solution.py:835
  249.4 1.6 collective-permute-done.38.refs_2_
  251.0 1.6 finish.1
  (167 shorter events, 18.7 us)
Async XLA Ops:
  7.3 82.7 %all-gather.3.cloned.1.call-start = ((), (), s32[]{:S(2)}) async-start(), calls=%async_computation | async-start | bytes 4866048 | tf_op jit(solution)/shard_map/all_gather | solution.py:1171
  9.9 9.6 %collective-permute-start = (bf16[208,384]{1,0:T(8,128)(2,1)S(1)}, bf16[208,384]{1,0:T(8,128)(2,1)S(1)}, u32[]{:S(2)}, u32[]{:S(2)}) collective-permute-start(bf16[208,384]{1,0:T(8,128)(2,1)S(1)} %get-tuple-element.223), channel_id=1, source_target_pairs={{0,2},{1,3},{2,0},{3,1},{4,6},{5,7},{6,4},{7,5},{8,10},{9,11},{10,... | collective-permute-start | bytes 479240 | tf_op jit(solution)/shard_map/ppermute | solution.py:839
  13.0 15.8 %collective-permute-start.1 = (bf16[208,384]{1,0:T(8,128)(2,1)S(1)}, bf16[208,384]{1,0:T(8,128)(2,1)S(1)}, u32[]{:S(2)}, u32[]{:S(2)}) collective-permute-start(bf16[208,384]{1,0:T(8,128)(2,1)S(1)} %get-tuple-element.223), channel_id=1, source_target_pairs={{0,4},{1,5},{2,6},{3,7},{4,0},{5,1},{6,2},{7,3},{8,12},{9,13},{10,... | collective-permute-start | bytes 479240 | tf_op jit(solution)/shard_map/ppermute | solution.py:839
  15.5 13.3 %collective-permute-start.2 = (bf16[208,384]{1,0:T(8,128)(2,1)S(1)}, bf16[208,384]{1,0:T(8,128)(2,1)S(1)}, u32[]{:S(2)}, u32[]{:S(2)}) collective-permute-start(bf16[208,384]{1,0:T(8,128)(2,1)S(1)} %get-tuple-element.223), channel_id=1, source_target_pairs={{0,6},{1,7},{2,4},{3,5},{4,2},{5,3},{6,0},{7,1},{8,14},{9,15},{10,... | collective-permute-start | bytes 479240 | tf_op jit(solution)/shard_map/ppermute | solution.py:839
  28.9 13.8 %copy-start.5 = (f32[96,3072]{1,0:T(8,128)S(1)}, f32[96,3072]{1,0:T(8,128)}, u32[]{:S(2)}) copy-start(f32[96,3072]{1,0:T(8,128)} %param.29) | copy-start | bytes 3538948
  28.9 12.1 %collective-permute-start.3 = (bf16[4,208,384]{2,1,0:T(8,128)(2,1)S(1)}, bf16[4,208,384]{2,1,0:T(8,128)(2,1)S(1)}, u32[]{:S(2)}, u32[]{:S(2)}) collective-permute-start(bf16[4,208,384]{2,1,0:T(8,128)(2,1)S(1)} %pad_maximum_fusion), channel_id=1, source_target_pairs={{0,16},{1,17},{2,18},{3,19},{4,20},{5,21},{6,22},{7,23},{8,9},{9,8... | collective-permute-start | bytes 1916936 | tf_op jit(solution)/shard_map/ppermute | solution.py:843
  41.1 21.5 %copy-start.8 = (bf16[8,208,384]{2,1,0:T(8,128)(2,1)}, bf16[8,208,384]{2,1,0:T(8,128)(2,1)S(1)}, u32[]{:S(2)}) copy-start(bf16[8,208,384]{2,1,0:T(8,128)(2,1)S(1)} %constant_dynamic-update-slice_fusion.refs_5_) | copy-start | bytes 3833860
  41.1 21.2 %collective-permute-start.7 = (bf16[8,208,384]{2,1,0:T(8,128)(2,1)S(1)}, bf16[8,208,384]{2,1,0:T(8,128)(2,1)}, u32[]{:S(2)}, u32[]{:S(2)}) collective-permute-start(bf16[8,208,384]{2,1,0:T(8,128)(2,1)S(1)} %constant_dynamic-update-slice_fusion.refs_5_), channel_id=1, source_target_pairs={{0,1},{1,0},{2,3},{3,2},{4,5},{5,4},{6,7},{7,6},{8,24},{9,25},{10,... | collective-permute-start | bytes 3833864 | tf_op jit(solution)/shard_map/ppermute | solution.py:843
  42.7 19.7 %collective-permute-start.8 = (bf16[8,208,384]{2,1,0:T(8,128)(2,1)S(1)}, bf16[8,208,384]{2,1,0:T(8,128)(2,1)S(1)}, u32[]{:S(2)}, u32[]{:S(2)}) collective-permute-start(bf16[8,208,384]{2,1,0:T(8,128)(2,1)S(1)} %constant_dynamic-update-slice_fusion.refs_5_), channel_id=1, source_target_pairs={{0,8},{1,9},{2,10},{3,11},{4,12},{5,13},{6,14},{7,15},{8,0},{9,1},... | collective-permute-start | bytes 3833864 | tf_op jit(solution)/shard_map/ppermute | solution.py:831
  42.8 13.9 %collective-permute-start.4 = (bf16[48,1536]{1,0:T(8,128)(2,1)S(1)}, bf16[48,1536]{1,0:T(8,128)(2,1)S(1)}, u32[]{:S(2)}, u32[]{:S(2)}) collective-permute-start(bf16[48,1536]{1,0:T(8,128)(2,1)S(1)} %fusion.2), channel_id=1, source_target_pairs={{0,2},{1,3},{2,0},{3,1},{4,6},{5,7},{6,4},{7,5},{8,10},{9,11},{10,... | collective-permute-start | bytes 442376 | tf_op jit(solution)/shard_map/ppermute | solution.py:839
  45.3 11.9 %collective-permute-start.5 = (bf16[48,1536]{1,0:T(8,128)(2,1)S(1)}, bf16[48,1536]{1,0:T(8,128)(2,1)S(1)}, u32[]{:S(2)}, u32[]{:S(2)}) collective-permute-start(bf16[48,1536]{1,0:T(8,128)(2,1)S(1)} %fusion.2), channel_id=1, source_target_pairs={{0,4},{1,5},{2,6},{3,7},{4,0},{5,1},{6,2},{7,3},{8,12},{9,13},{10,... | collective-permute-start | bytes 442376 | tf_op jit(solution)/shard_map/ppermute | solution.py:839
  47.1 15.2 %collective-permute-start.6 = (bf16[48,1536]{1,0:T(8,128)(2,1)S(1)}, bf16[48,1536]{1,0:T(8,128)(2,1)S(1)}, u32[]{:S(2)}, u32[]{:S(2)}) collective-permute-start(bf16[48,1536]{1,0:T(8,128)(2,1)S(1)} %fusion.2), channel_id=1, source_target_pairs={{0,6},{1,7},{2,4},{3,5},{4,2},{5,3},{6,0},{7,1},{8,14},{9,15},{10,... | collective-permute-start | bytes 442376 | tf_op jit(solution)/shard_map/ppermute | solution.py:839
  62.2 5.2 %copy-start.3 = (s32[8]{0:T(128)S(1)}, s32[8]{0:T(128)}, u32[]{:S(2)}) copy-start(s32[8]{0:T(128)} %refs_1_.4) | copy-start | bytes 100
  62.3 5.2 %copy-start.4 = (s32[8]{0:T(128)S(1)}, s32[8]{0:T(128)}, u32[]{:S(2)}) copy-start(s32[8]{0:T(128)} %refs_2_.4) | copy-start | bytes 100
  62.4 3.4 %collective-permute-start.9 = (bf16[8,208,384]{2,1,0:T(8,128)(2,1)}, bf16[8,208,384]{2,1,0:T(8,128)(2,1)}, u32[]{:S(2)}, u32[]{:S(2)}) collective-permute-start(bf16[8,208,384]{2,1,0:T(8,128)(2,1)} %collective-permute-done.7.refs_6_), channel_id=1, source_target_pairs={{0,8},{1,9},{2,10},{3,11},{4,12},{5,13},{6,14},{7,15},{8,0},{9,1},... | collective-permute-start | bytes 3833864 | tf_op jit(solution)/shard_map/ppermute | solution.py:831
  63.5 22.5 %collective-permute-start.10 = (bf16[4,48,1536]{2,1,0:T(8,128)(2,1)S(1)}, bf16[4,48,1536]{2,1,0:T(8,128)(2,1)S(1)}, u32[]{:S(2)}, u32[]{:S(2)}) collective-permute-start(bf16[4,48,1536]{2,1,0:T(8,128)(2,1)S(1)} %pad_maximum_fusion.1.refs_9_), channel_id=1, source_target_pairs={{0,16},{1,17},{2,18},{3,19},{4,20},{5,21},{6,22},{7,23},{8,9},{9,8... | collective-permute-start | bytes 1769480 | tf_op jit(solution)/shard_map/ppermute | solution.py:843
  86.0 16.4 %copy-start = (bf16[8,48,1536]{2,1,0:T(8,128)(2,1)}, bf16[8,48,1536]{2,1,0:T(8,128)(2,1)S(1)}, u32[]{:S(2)}) copy-start(bf16[8,48,1536]{2,1,0:T(8,128)(2,1)S(1)} %constant_dynamic-update-slice_fusion.5.refs_4_.refs_8_) | copy-start | bytes 3538948
  86.0 16.7 %collective-permute-start.11 = (bf16[8,48,1536]{2,1,0:T(8,128)(2,1)S(1)}, bf16[8,48,1536]{2,1,0:T(8,128)(2,1)}, u32[]{:S(2)}, u32[]{:S(2)}) collective-permute-start(bf16[8,48,1536]{2,1,0:T(8,128)(2,1)S(1)} %constant_dynamic-update-slice_fusion.5.refs_4_.refs_8_), channel_id=1, source_target_pairs={{0,1},{1,0},{2,3},{3,2},{4,5},{5,4},{6,7},{7,6},{8,24},{9,25},{10,... | collective-permute-start | bytes 3538952 | tf_op jit(solution)/shard_map/ppermute | solution.py:843
  102.4 2.9 %collective-permute-start.12 = (bf16[8,48,1536]{2,1,0:T(8,128)(2,1)S(1)}, bf16[8,48,1536]{2,1,0:T(8,128)(2,1)S(1)}, u32[]{:S(2)}, u32[]{:S(2)}) collective-permute-start(bf16[8,48,1536]{2,1,0:T(8,128)(2,1)S(1)} %constant_dynamic-update-slice_fusion.5.refs_4_.refs_8_), channel_id=1, source_target_pairs={{0,8},{1,9},{2,10},{3,11},{4,12},{5,13},{6,14},{7,15},{8,0},{9,1},... | collective-permute-start | bytes 3538952 | tf_op jit(solution)/shard_map/ppermute | solution.py:831
  102.8 4.5 %collective-permute-start.13 = (bf16[8,48,1536]{2,1,0:T(8,128)(2,1)}, bf16[8,48,1536]{2,1,0:T(8,128)(2,1)S(1)}, u32[]{:S(2)}, u32[]{:S(2)}) collective-permute-start(bf16[8,48,1536]{2,1,0:T(8,128)(2,1)} %collective-permute-done.11.refs_9_), channel_id=1, source_target_pairs={{0,8},{1,9},{2,10},{3,11},{4,12},{5,13},{6,14},{7,15},{8,0},{9,1},... | collective-permute-start | bytes 3538952 | tf_op jit(solution)/shard_map/ppermute | solution.py:831
  127.8 5.7 %collective-permute-start.14 = (bf16[16,192,384]{2,1,0:T(8,128)(2,1)}, bf16[16,192,384]{2,1,0:T(8,128)(2,1)S(1)}, u32[]{:S(2)}, u32[]{:S(2)}) collective-permute-start(bf16[16,192,384]{2,1,0:T(8,128)(2,1)} %get-tuple-element.133), channel_id=1, source_target_pairs={{0,8},{1,9},{2,10},{3,11},{4,12},{5,13},{6,14},{7,15},{8,0},{9,1},... | collective-permute-start | bytes 7077896 | tf_op jit(solution)/shard_map/ppermute | solution.py:831
  134.0 16.5 %collective-permute-start.15 = (bf16[1536,384]{1,0:T(8,128)(2,1)S(1)}, bf16[1536,384]{1,0:T(8,128)(2,1)S(1)}, u32[]{:S(2)}, u32[]{:S(2)}) collective-permute-start(bf16[1536,384]{1,0:T(8,128)(2,1)S(1)} %get-tuple-element.143), channel_id=1, source_target_pairs={{0,1},{1,0},{2,3},{3,2},{4,5},{5,4},{6,7},{7,6},{8,24},{9,25},{10,... | collective-permute-start | bytes 3538952 | tf_op jit(solution)/shard_map/ppermute | solution.py:843
  150.9 10.6 %collective-permute-start.17 = (bf16[16,192,384]{2,1,0:T(8,128)(2,1)S(1)}, bf16[16,192,384]{2,1,0:T(8,128)(2,1)S(1)}, u32[]{:S(2)}, u32[]{:S(2)}) collective-permute-start(bf16[16,192,384]{2,1,0:T(8,128)(2,1)S(1)} %copy-done.19), channel_id=1, source_target_pairs={{0,8},{1,9},{2,10},{3,11},{4,12},{5,13},{6,14},{7,15},{8,0},{9,1},... | collective-permute-start | bytes 7077896 | tf_op jit(solution)/shard_map/ppermute | solution.py:831
  150.9 11.8 %collective-permute-start.16 = (bf16[768,384]{1,0:T(8,128)(2,1)S(1)}, bf16[768,384]{1,0:T(8,128)(2,1)S(1)}, u32[]{:S(2)}, u32[]{:S(2)}) collective-permute-start(bf16[768,384]{1,0:T(8,128)(2,1)S(1)} %get-tuple-element.153), channel_id=1, source_target_pairs={{0,16},{1,17},{2,18},{3,19},{4,20},{5,21},{6,22},{7,23},{8,9},{9,8... | collective-permute-start | bytes 1769480 | tf_op jit(solution)/shard_map/ppermute | solution.py:843
  162.0 19.8 %collective-permute-start.18 = (bf16[1536,384]{1,0:T(8,128)(2,1)S(1)}, bf16[1536,384]{1,0:T(8,128)(2,1)S(1)}, u32[]{:S(2)}, u32[]{:S(2)}) collective-permute-start(bf16[1536,384]{1,0:T(8,128)(2,1)S(1)} %get-tuple-element.167), channel_id=1, source_target_pairs={{0,1},{1,0},{2,3},{3,2},{4,5},{5,4},{6,7},{7,6},{8,24},{9,25},{10,... | collective-permute-start | bytes 3538952 | tf_op jit(solution)/shard_map/ppermute | solution.py:843
  162.9 21.4 %collective-permute-start.19 = (bf16[192,384]{1,0:T(8,128)(2,1)S(1)}, bf16[192,384]{1,0:T(8,128)(2,1)S(1)}, u32[]{:S(2)}, u32[]{:S(2)}) collective-permute-start(bf16[192,384]{1,0:T(8,128)(2,1)S(1)} %get-tuple-element.172), channel_id=1, source_target_pairs={{0,2},{1,3},{2,0},{3,1},{4,6},{5,7},{6,4},{7,5},{8,10},{9,11},{10,... | collective-permute-start | bytes 442376 | tf_op jit(solution)/shard_map/ppermute | solution.py:839
  164.8 19.5 %collective-permute-start.20 = (bf16[192,384]{1,0:T(8,128)(2,1)S(1)}, bf16[192,384]{1,0:T(8,128)(2,1)S(1)}, u32[]{:S(2)}, u32[]{:S(2)}) collective-permute-start(bf16[192,384]{1,0:T(8,128)(2,1)S(1)} %get-tuple-element.173), channel_id=1, source_target_pairs={{0,4},{1,5},{2,6},{3,7},{4,0},{5,1},{6,2},{7,3},{8,12},{9,13},{10,... | collective-permute-start | bytes 442376 | tf_op jit(solution)/shard_map/ppermute | solution.py:839
  165.5 18.8 %collective-permute-start.21 = (bf16[192,384]{1,0:T(8,128)(2,1)S(1)}, bf16[192,384]{1,0:T(8,128)(2,1)S(1)}, u32[]{:S(2)}, u32[]{:S(2)}) collective-permute-start(bf16[192,384]{1,0:T(8,128)(2,1)S(1)} %get-tuple-element.174), channel_id=1, source_target_pairs={{0,6},{1,7},{2,4},{3,5},{4,2},{5,3},{6,0},{7,1},{8,14},{9,15},{10,... | collective-permute-start | bytes 442376 | tf_op jit(solution)/shard_map/ppermute | solution.py:839
  167.4 13.7 %copy-start.1 = (f32[3,32,16]{2,1,0:T(8,128)S(1)}, f32[3,32,16]{2,1,0:T(8,128)}, u32[]{:S(2)}) copy-start(f32[3,32,16]{2,1,0:T(8,128)} %constant.117.clone.refs_1_) | copy-start | bytes 18436
  167.4 13.7 %copy-start.2 = (f32[3,32,8]{2,1,0:T(8,128)S(1)}, f32[3,32,8]{2,1,0:T(8,128)}, u32[]{:S(2)}) copy-start(f32[3,32,8]{2,1,0:T(8,128)} %constant.118.clone.refs_2_) | copy-start | bytes 9220
  181.8 10.3 %collective-permute-start.22 = (bf16[16,384]{1,0:T(8,128)(2,1)S(1)}, bf16[16,384]{1,0:T(8,128)(2,1)S(1)}, u32[]{:S(2)}, u32[]{:S(2)}) collective-permute-start(bf16[16,384]{1,0:T(8,128)(2,1)S(1)} %get-tuple-element.171.refs_6_), channel_id=1, source_target_pairs={{0,8},{1,9},{2,10},{3,11},{4,12},{5,13},{6,14},{7,15},{8,0},{9,1},... | collective-permute-start | bytes 36872 | tf_op jit(solution)/shard_map/ppermute | solution.py:831
  182.2 9.9 %collective-permute-start.23 = (bf16[768,384]{1,0:T(8,128)(2,1)S(1)}, bf16[768,384]{1,0:T(8,128)(2,1)S(1)}, u32[]{:S(2)}, u32[]{:S(2)}) collective-permute-start(bf16[768,384]{1,0:T(8,128)(2,1)S(1)} %get-tuple-element.177), channel_id=1, source_target_pairs={{0,16},{1,17},{2,18},{3,19},{4,20},{5,21},{6,22},{7,23},{8,9},{9,8... | collective-permute-start | bytes 1769480 | tf_op jit(solution)/shard_map/ppermute | solution.py:843
  184.3 8.1 %copy-start.11 = (pred[16]{0:T(512)(128)(4,1)S(1)}, pred[16]{0:T(512)(128)(4,1)}, u32[]{:S(2)}) copy-start(pred[16]{0:T(512)(128)(4,1)} %constant.116.clone.1) | copy-start | bytes 52
  192.2 4.8 %collective-permute-start.24 = (bf16[16,192,384]{2,1,0:T(8,128)(2,1)}, bf16[16,192,384]{2,1,0:T(8,128)(2,1)S(1)}, u32[]{:S(2)}, u32[]{:S(2)}) collective-permute-start(bf16[16,192,384]{2,1,0:T(8,128)(2,1)} %get-tuple-element.180), channel_id=1, source_target_pairs={{0,8},{1,9},{2,10},{3,11},{4,12},{5,13},{6,14},{7,15},{8,0},{9,1},... | collective-permute-start | bytes 7077896 | tf_op jit(solution)/shard_map/ppermute | solution.py:831
  192.5 21.1 %collective-permute-start.27 = (bf16[192,384]{1,0:T(8,128)(2,1)S(1)}, bf16[192,384]{1,0:T(8,128)(2,1)S(1)}, u32[]{:S(2)}, u32[]{:S(2)}) collective-permute-start(bf16[192,384]{1,0:T(8,128)(2,1)S(1)} %get-tuple-element.190), channel_id=1, source_target_pairs={{0,2},{1,3},{2,0},{3,1},{4,6},{5,7},{6,4},{7,5},{8,10},{9,11},{10,... | collective-permute-start | bytes 442376 | tf_op jit(solution)/shard_map/ppermute | solution.py:839
  193.4 20.2 %collective-permute-start.28 = (bf16[192,384]{1,0:T(8,128)(2,1)S(1)}, bf16[192,384]{1,0:T(8,128)(2,1)S(1)}, u32[]{:S(2)}, u32[]{:S(2)}) collective-permute-start(bf16[192,384]{1,0:T(8,128)(2,1)S(1)} %get-tuple-element.191), channel_id=1, source_target_pairs={{0,4},{1,5},{2,6},{3,7},{4,0},{5,1},{6,2},{7,3},{8,12},{9,13},{10,... | collective-permute-start | bytes 442376 | tf_op jit(solution)/shard_map/ppermute | solution.py:839
  194.9 18.6 %collective-permute-start.29 = (bf16[192,384]{1,0:T(8,128)(2,1)S(1)}, bf16[192,384]{1,0:T(8,128)(2,1)S(1)}, u32[]{:S(2)}, u32[]{:S(2)}) collective-permute-start(bf16[192,384]{1,0:T(8,128)(2,1)S(1)} %get-tuple-element.192), channel_id=1, source_target_pairs={{0,6},{1,7},{2,4},{3,5},{4,2},{5,3},{6,0},{7,1},{8,14},{9,15},{10,... | collective-permute-start | bytes 442376 | tf_op jit(solution)/shard_map/ppermute | solution.py:839
  197.6 6.7 %collective-permute-start.26 = (bf16[192,384]{1,0:T(8,128)(2,1)S(1)}, bf16[192,384]{1,0:T(8,128)(2,1)S(1)}, u32[]{:S(2)}, u32[]{:S(2)}) collective-permute-start(bf16[192,384]{1,0:T(8,128)(2,1)S(1)} %total.3.refs_4_), channel_id=1, source_target_pairs={{0,16},{1,17},{2,18},{3,19},{4,20},{5,21},{6,22},{7,23},{8,24},{9,... | collective-permute-start | bytes 442376 | tf_op jit(solution)/shard_map/ppermute | solution.py:835
  199.6 16.3 %collective-permute-start.25 = (bf16[1552,384]{1,0:T(8,128)(2,1)S(1)}, bf16[1552,384]{1,0:T(8,128)(2,1)S(1)}, u32[]{:S(2)}, u32[]{:S(2)}) collective-permute-start(bf16[1552,384]{1,0:T(8,128)(2,1)S(1)} %get-tuple-element.188), channel_id=1, source_target_pairs={{0,1},{1,0},{2,3},{3,2},{4,5},{5,4},{6,7},{7,6},{8,24},{9,25},{10,... | collective-permute-start | bytes 3575816 | tf_op jit(solution)/shard_map/ppermute | solution.py:843
  204.5 12.1 %collective-permute-start.33 = (bf16[48,3072]{1,0:T(8,128)(2,1)S(1)}, bf16[48,3072]{1,0:T(8,128)(2,1)S(1)}, u32[]{:S(2)}, u32[]{:S(2)}) collective-permute-start(bf16[48,3072]{1,0:T(8,128)(2,1)S(1)} %pad_maximum_fusion.4), channel_id=1, source_target_pairs={{0,8},{1,9},{2,10},{3,11},{4,12},{5,13},{6,14},{7,15},{8,0},{9,1},... | collective-permute-start | bytes 884744 | tf_op jit(solution)/shard_map/ppermute | solution.py:831
  216.4 6.2 %collective-permute-start.31 = (bf16[192,384]{1,0:T(8,128)(2,1)S(1)}, bf16[192,384]{1,0:T(8,128)(2,1)S(1)}, u32[]{:S(2)}, u32[]{:S(2)}) collective-permute-start(bf16[192,384]{1,0:T(8,128)(2,1)S(1)} %total.4), channel_id=1, source_target_pairs={{0,16},{1,17},{2,18},{3,19},{4,20},{5,21},{6,22},{7,23},{8,24},{9,... | collective-permute-start | bytes 442376 | tf_op jit(solution)/shard_map/ppermute | solution.py:835
  216.6 12.4 %collective-permute-start.30 = (bf16[784,384]{1,0:T(8,128)(2,1)S(1)}, bf16[784,384]{1,0:T(8,128)(2,1)S(1)}, u32[]{:S(2)}, u32[]{:S(2)}) collective-permute-start(bf16[784,384]{1,0:T(8,128)(2,1)S(1)} %get-tuple-element.194), channel_id=1, source_target_pairs={{0,16},{1,17},{2,18},{3,19},{4,20},{5,21},{6,22},{7,23},{8,9},{9,8... | collective-permute-start | bytes 1806344 | tf_op jit(solution)/shard_map/ppermute | solution.py:843
  222.7 11.4 %collective-permute-start.32 = (bf16[192,768]{1,0:T(8,128)(2,1)S(1)}, bf16[192,768]{1,0:T(8,128)(2,1)S(1)}, u32[]{:S(2)}, u32[]{:S(2)}) collective-permute-start(bf16[192,768]{1,0:T(8,128)(2,1)S(1)} %pad_maximum_fusion.3), channel_id=1, source_target_pairs={{0,8},{1,9},{2,10},{3,11},{4,12},{5,13},{6,14},{7,15},{8,0},{9,1},... | collective-permute-start | bytes 884744 | tf_op jit(solution)/shard_map/ppermute | solution.py:831
  229.7 6.9 %collective-permute-start.34 = (bf16[208,384]{1,0:T(8,128)(2,1)S(1)}, bf16[208,384]{1,0:T(8,128)(2,1)S(1)}, u32[]{:S(2)}, u32[]{:S(2)}) collective-permute-start(bf16[208,384]{1,0:T(8,128)(2,1)S(1)} %get-tuple-element.199), channel_id=1, source_target_pairs={{0,2},{1,3},{2,0},{3,1},{4,6},{5,7},{6,4},{7,5},{8,10},{9,11},{10,... | collective-permute-start | bytes 479240 | tf_op jit(solution)/shard_map/ppermute | solution.py:839
  229.7 14.1 %collective-permute-start.35 = (bf16[208,384]{1,0:T(8,128)(2,1)S(1)}, bf16[208,384]{1,0:T(8,128)(2,1)S(1)}, u32[]{:S(2)}, u32[]{:S(2)}) collective-permute-start(bf16[208,384]{1,0:T(8,128)(2,1)S(1)} %get-tuple-element.200), channel_id=1, source_target_pairs={{0,4},{1,5},{2,6},{3,7},{4,0},{5,1},{6,2},{7,3},{8,12},{9,13},{10,... | collective-permute-start | bytes 479240 | tf_op jit(solution)/shard_map/ppermute | solution.py:839
  231.9 11.9 %collective-permute-start.36 = (bf16[208,384]{1,0:T(8,128)(2,1)S(1)}, bf16[208,384]{1,0:T(8,128)(2,1)S(1)}, u32[]{:S(2)}, u32[]{:S(2)}) collective-permute-start(bf16[208,384]{1,0:T(8,128)(2,1)S(1)} %get-tuple-element.201), channel_id=1, source_target_pairs={{0,6},{1,7},{2,4},{3,5},{4,2},{5,3},{6,0},{7,1},{8,14},{9,15},{10,... | collective-permute-start | bytes 479240 | tf_op jit(solution)/shard_map/ppermute | solution.py:839
  243.9 5.3 %collective-permute-start.37 = (bf16[208,384]{1,0:T(8,128)(2,1)S(1)}, bf16[208,384]{1,0:T(8,128)(2,1)S(1)}, u32[]{:S(2)}, u32[]{:S(2)}) collective-permute-start(bf16[208,384]{1,0:T(8,128)(2,1)S(1)} %total.5), channel_id=1, source_target_pairs={{0,16},{1,17},{2,18},{3,19},{4,20},{5,21},{6,22},{7,23},{8,24},{9,... | collective-permute-start | bytes 479240 | tf_op jit(solution)/shard_map/ppermute | solution.py:835
  249.3 1.7 collective-permute-start.38
  (13 other events, 31.0 us)
Sparse Core Ops, SparseCore 0:
  11.6 78.3 all-gather.2

commit v2 on v1

--- a/solution.py
+++ b/solution.py
@@ -1011,20 +1011,21 @@
         first += half
     mine = mine_ref[first : first + 16, :].astype(F32)[:1]
     other = other_ref[first : first + 16, :].astype(F32)[:1]
-    width = small_ref.shape[1]
-    for k, line in enumerate((jnp.where(c == 0, mine, other), jnp.where(c == 0, other, mine))):
-        small_ref[2 * k : 2 * k + 1, :] = line[:, :width]
-        small_ref[2 * k + 1 : 2 * k + 2, :] = line[:, width:]
-
-
-def finish(meta, mine, other, d):
+    side, quarter = mine.shape[1] // 2, small_ref.shape[1] // 4
+    parts = []
+    for line in (jnp.where(c == 0, mine, other), jnp.where(c == 0, other, mine)):
+        parts += [line[:, :quarter], line[:, side : side + quarter]]
+    small_ref[...] = jnp.concatenate(parts, axis=1)
+
+
+def finish(meta, mine, other, d, quarter):
     return kernel_call(
         finish_kernel,
         [],
         [SMEM, WHOLE, WHOLE],
         [meta, near(mine), near(other)],
         out_specs=[WHOLE] * 3,
-        out_shape=[HBM((3 * d // 8, d), F32), HBM((d // 8, d), F32), VMEM((4, d // 2), F32)],
+        out_shape=[HBM((3 * d // 8, d), F32), HBM((d // 8, d), F32), VMEM((1, 4 * quarter), F32)],
         name="finish",
     )
 
@@ -1290,8 +1291,8 @@
         qkv_total = qkv_sum.total()
         qkv_mine = side_by_side(qkv_total, to_x(qkv_total), x)
         qkv_other = to_core(qkv_mine)
-        grad_qkv, grad_out, small_all = finish(meta, qkv_mine, qkv_other, d)
-        small_total = small_all[:, :quarter].reshape(-1)
+        grad_qkv, grad_out, small_all = finish(meta, qkv_mine, qkv_other, d, quarter)
+        small_total = small_all.reshape(-1)
     else:
         tokens_grad, _ = tokens_back(attn_sum, grad_joined, wqkv)
 

time: 264 us -> 264 us (level)
  no operation moved by 1% of the time
where the time goes in v2:
time: 264 us; the launch traced here: 261 us
  Pallas kernels  112 us (42%)
  waiting for transfers between devices  80 us (30%)
  starting transfers between devices  43.4 us (16%)
  between operations  15 us (6%)
  other arithmetic  5.5 us (2%)
  local copies, waits for them, and re-layouts  4.8 us (2%)
    pallas_call x23, Pallas kernels, kernel_call(): return call(*args, *deps)  112 us
    ppermute x15, waiting for transfers between devices, to_z(): return lax.ppermute(v, AXES, route(lambda x, c, z, y: (x, c, z ^ k, y)))  35.5 us
    ppermute x15, starting transfers between devices, to_z(): return lax.ppermute(v, AXES, route(lambda x, c, z, y: (x, c, z ^ k, y)))  24.6 us
    ppermute x10, waiting for transfers between devices, to_cross(): lax.ppermute(v, AXES, route(lambda x, c, z, y: (1 - x, c, z, y) if c == f...  22.2 us
    ppermute x10, starting transfers between devices, to_cross(): lax.ppermute(v, AXES, route(lambda x, c, z, y: (1 - x, c, z, y) if c == f...  14.5 us
    ppermute x3, waiting for transfers between devices, to_x(): return lax.ppermute(v, AXES, route(lambda x, c, z, y: (1 - x, c, z, y)))  13.1 us
    ppermute x11, waiting for transfers between devices, to_core(): return lax.ppermute(v, AXES, route(lambda x, c, z, y: (x, 1 - c, z, y)))  6.13 us
  transfers between devices with their start and end apart: 40, of which 20 were waited for; matrix products, arithmetic and copies ran while one was open for 2% of the time, Pallas kernels for 34%

profile of v2, /device:TPU:0, one launch (start us, length us, event | category | flops | bytes accessed | tf_op | source)
XLA Modules:
  0.0 261.5 jit_solution(612946247417814231)
XLA Ops:
  7.4 1.4 slice_select_fusion
  9.9 3.1 %collective-permute-start = (bf16[208,384]{1,0:T(8,128)(2,1)S(1)}, bf16[208,384]{1,0:T(8,128)(2,1)S(1)}, u32[]{:S(2)}, u32[]{:S(2)}) collective-permute-start(bf16[208,384]{1,0:T(8,128)(2,1)S(1)} %get-tuple-element.223), channel_id=1, source_target_pairs={{0,2},{1,3},{2,0},{3,1},{4,6},{5,7},{6,4},{7,5},{8,10},{9,11},{10,... | collective-permute-start | bytes 479240 | tf_op jit(solution)/shard_map/ppermute | solution.py:839
  13.0 2.6 collective-permute-start.1
  15.6 3.9 %collective-permute-done = bf16[208,384]{1,0:T(8,128)(2,1)S(1)} collective-permute-done((bf16[208,384]{1,0:T(8,128)(2,1)S(1)}, bf16[208,384]{1,0:T(8,128)(2,1)S(1)}, u32[]{:S(2)}, u32[]{:S(2)}) %collective-permute-start) | collective-permute-done | bytes 159776 | tf_op jit(solution)/shard_map/ppermute | solution.py:839
  19.4 9.4 %collective-permute-done.1 = bf16[208,384]{1,0:T(8,128)(2,1)S(1)} collective-permute-done((bf16[208,384]{1,0:T(8,128)(2,1)S(1)}, bf16[208,384]{1,0:T(8,128)(2,1)S(1)}, u32[]{:S(2)}, u32[]{:S(2)}) %collective-permute-start.1) | collective-permute-done | bytes 159776 | tf_op jit(solution)/shard_map/ppermute | solution.py:839
  28.9 1.6 collective-permute-start.3
  30.6 10.4 %collective-permute-done.3 = bf16[4,208,384]{2,1,0:T(8,128)(2,1)S(1)} collective-permute-done((bf16[4,208,384]{2,1,0:T(8,128)(2,1)S(1)}, bf16[4,208,384]{2,1,0:T(8,128)(2,1)S(1)}, u32[]{:S(2)}, u32[]{:S(2)}) %collective-permute-start.3) | collective-permute-done | bytes 639008 | tf_op jit(solution)/shard_map/ppermute | solution.py:843
  41.1 1.6 collective-permute-start.7
  42.8 2.5 collective-permute-start.4
  45.3 1.8 collective-permute-start.5
  47.1 1.4 collective-permute-start.6
  48.5 8.2 %collective-permute-done.4 = bf16[48,1536]{1,0:T(8,128)(2,1)S(1)} collective-permute-done((bf16[48,1536]{1,0:T(8,128)(2,1)S(1)}, bf16[48,1536]{1,0:T(8,128)(2,1)S(1)}, u32[]{:S(2)}, u32[]{:S(2)}) %collective-permute-start.4) | collective-permute-done | bytes 147488 | tf_op jit(solution)/shard_map/ppermute | solution.py:839
  57.2 5.0 %collective-permute-done.6 = bf16[48,1536]{1,0:T(8,128)(2,1)S(1)} collective-permute-done((bf16[48,1536]{1,0:T(8,128)(2,1)S(1)}, bf16[48,1536]{1,0:T(8,128)(2,1)S(1)}, u32[]{:S(2)}, u32[]{:S(2)}) %collective-permute-start.6) | collective-permute-done | bytes 147488 | tf_op jit(solution)/shard_map/ppermute | solution.py:839
  63.5 2.0 collective-permute-start.10
  67.5 18.5 %attention_forward.1 = (bf16[1024,2304]{1,0:T(8,128)(2,1)}, bf16[8,6,128,256]{3,2,1,0:T(8,128)(2,1)}, bf16[1024,768]{1,0:T(8,128)(2,1)}, bf16[1024,768]{1,0:T(8,...) custom-call(s32[4]{0:T(128)S(1)} %pad_add_fusion.refs_0_, ...), custom_call_target="tpu_custom_call" | custom-call | flops 4831838208 | bytes 12582912 | tf_op jit(solution)/shard_map/attention_forward/pallas_call | solution.py:62
  86.9 3.0 %all-gather.3.cloned.1.call-done = bf16[6144,384]{1,0:T(8,128)(2,1)} async-done(((bf16[192,384]{1,0:T(8,128)(2,1)}), bf16[6144,384]{1,0:T(8,128)(2,1)}) %all-gather.3.cloned.1.call-update) | async-done | bytes 4718608 | tf_op jit(solution)/shard_map/all_gather | solution.py:1172
  90.0 12.4 %up_forward.1 = (bf16[1024,3072]{1,0:T(8,128)(2,1)S(1)}, bf16[1024,3072]{1,0:T(8,128)(2,1)S(1)}, f32[8,128]{1,0:T(8,128)}) custom-call(s32[4]{0:T(128)S(1)} %pad_add_fusion.refs_0_, bf16[1024,768]{1,0:T(8,128)(2,1)} %get-tuple-element.116.refs_1_.refs_2_, f32[1,3072]{1,0:T(1,128)S(1)} %bitcast.49, bf16[32,192,384]{2,1,0:T(8,128)(2,1)} %bitcast.60, ...), custom_call_target="tpu_custom_call" | custom-call | flops 9663676416 | bytes 12582912 | tf_op jit(solution)/shard_map/up_forward/pallas_call | solution.py:62
  103.0 2.3 collective-permute-done.12.refs_10_
  105.3 1.9 collective-permute-done.13.refs_11_
  107.2 20.5 %down_forward.1 = (bf16[1024,768]{1,0:T(8,128)(2,1)}, f32[1024,768]{1,0:T(8,128)}, bf16[1024,768]{1,0:T(8,128)(2,1)S(1)}, f32[8,768]{1,0:T(8,128)S(1)}, bf16[768...) custom-call(s32[4]{0:T(128)S(1)} %pad_add_fusion.refs_0_, ...), custom_call_target="tpu_custom_call", output_to_operand_aliasing={{5}: (4, {})} | custom-call | flops 28991029248 | bytes 6291456 | tf_op jit(solution)/shard_map/down_forward/pallas_call | solution.py:62
  128.1 5.4 %hidden_grad.1 = (bf16[1024,3072]{1,0:T(8,128)(2,1)S(1)}, f32[1,3072]{1,0:T(1,128)S(1)}) custom-call(bf16[1024,768]{1,0:T(8,128)(2,1)S(1)} %get-tuple-element.126.refs_0_, bf16[1024,3072]{1,0:T(8,128)(2,1)S(1)} %get-tuple-element.127.refs_1_, bf16[768,3072]{1,0:T(8,128)(2,1)S(1)} %get-tuple-element.128.refs_2_), custom_call_target="tpu_custom_call" | custom-call | flops 9663676416 | bytes 12582912 | tf_op jit(solution)/shard_map/hidden_grad/pallas_call | solution.py:62
  134.0 2.3 collective-permute-start.15
  136.4 10.0 %up_grad.1 = (bf16[16,192,384]{2,1,0:T(8,128)(2,1)S(1)}, bf16[16,192,384]{2,1,0:T(8,128)(2,1)}, f32[8,128]{1,0:T(8,128)S(1)}, bf16[1024,3072]{1,0:T(8,128)(2,1)S...) custom-call(s32[4]{0:T(128)S(1)} %pad_add_fusion.refs_0_, ...), custom_call_target="tpu_custom_call", output_to_operand_aliasing={{3}: (1, {})} | custom-call | flops 9663676416 | bytes 6291456 | tf_op jit(solution)/shard_map/up_grad/pallas_call | solution.py:62
  146.4 4.1 %collective-permute-done.15.refs_1_ = bf16[1536,384]{1,0:T(8,128)(2,1)S(1)} collective-permute-done((bf16[1536,384]{1,0:T(8,128)(2,1)S(1)}, bf16[1536,384]{1,0:T(8,128)(2,1)S(1)}, u32[]{:S(2)}, u32[]{:S(2)}) %collective-permute-start.15) | collective-permute-done | bytes 1179680 | tf_op jit(solution)/shard_map/ppermute | solution.py:843
  150.9 1.5 collective-permute-start.16
  152.5 9.0 %first_back.1 = (f32[1024,768]{1,0:T(8,128)}, bf16[1024,768]{1,0:T(8,128)(2,1)}, bf16[1024,768]{1,0:T(8,128)(2,1)S(1)}, f32[8,768]{1,0:T(8,128)S(1)}) custom-call(f32[1024,768]{1,0:T(8,128)S(1)} %get-tuple-element.136.refs_0_, bf16[1024,3072]{1,0:T(8,128)(2,1)S(1)} %get-tuple-element.137.refs_1_, bf16[3072,768]{1,0:T(8,128)(2,1)S(1)} %get-tuple-element.138.refs_2_, ...), custom_call_target="tpu_custom_call" | custom-call | flops 9663676416 | bytes 6291456 | tf_op jit(solution)/shard_map/first_back/pallas_call | solution.py:62
  162.9 1.9 collective-permute-start.19
  165.4 1.9 collective-permute-start.21
  167.3 13.7 %attention_back.1 = (bf16[1024,2304]{1,0:T(8,128)(2,1)}, f32[8,768]{1,0:T(8,128)S(1)}, bf16[1024,2304]{1,0:T(8,128)(2,1)S(1)}, bf16[1024,768]{1,0:T(8,128)(2,1)S...) custom-call(bf16[1024,768]{1,0:T(8,128)(2,1)S(1)} %get-tuple-element.147.refs_0_, ...), custom_call_target="tpu_custom_call" | custom-call | flops 9663676416 | bytes 23592960 | tf_op jit(solution)/shard_map/attention_back/pallas_call | solution.py:62
  182.2 2.1 collective-permute-start.23
  184.3 7.8 %qkv_grad.1 = (bf16[16,192,384]{2,1,0:T(8,128)(2,1)S(1)}, bf16[16,192,384]{2,1,0:T(8,128)(2,1)}, f32[8,128]{1,0:T(8,128)}) custom-call(s32[4]{0:T(128)S(1)} %pad_add_fusion.refs_0_, bf16[1024,2304]{1,0:T(8,128)(2,1)S(1)} %get-tuple-element.162.refs_1_, bf16[1024,768]{1,0:T(8,128)(2,1)S(1)} %get-tuple-element.163.refs_2_, ...), custom_call_target="tpu_custom_call" | custom-call | flops 9663676416 | bytes 12582912 | tf_op jit(solution)/shard_map/qkv_grad/pallas_call | solution.py:62
  193.4 1.6 collective-permute-start.28
  194.9 2.0 collective-permute-start.29
  197.6 2.0 collective-permute-start.26
  199.8 4.5 %collective-permute-done.26.refs_4_ = bf16[192,384]{1,0:T(8,128)(2,1)S(1)} collective-permute-done((bf16[192,384]{1,0:T(8,128)(2,1)S(1)}, bf16[192,384]{1,0:T(8,128)(2,1)S(1)}, u32[]{:S(2)}, u32[]{:S(2)}) %collective-permute-start.26) | collective-permute-done | bytes 147488 | tf_op jit(solution)/shard_map/ppermute | solution.py:835
  204.5 9.0 %tokens_back.1 = (f32[1024,768]{1,0:T(8,128)}, f32[8,128]{1,0:T(8,128)S(1)}) custom-call(f32[1024,768]{1,0:T(8,128)} %get-tuple-element.146.refs_0_, bf16[1024,2304]{1,0:T(8,128)(2,1)} %get-tuple-element.160.refs_1_, bf16[2304,768]{1,0:T(8,128)(2,1)} %get-tuple-element.161.refs_2_, f32[8,128]{1,0:T(8,128)S(1)} %get-tuple-element.184.refs_4_.refs_3_, ...), custom_call_target="tpu_custom_call" | custom-call | flops 7247757312 | bytes 11010048 | tf_op jit(solution)/shard_map/tokens_back/pallas_call | solution.py:62
  213.5 2.4 collective-permute-done.25.refs_1_
  216.6 2.0 collective-permute-start.30
  218.6 4.0 %collective-permute-done.31.refs_3_ = bf16[192,384]{1,0:T(8,128)(2,1)S(1)} collective-permute-done((bf16[192,384]{1,0:T(8,128)(2,1)S(1)}, bf16[192,384]{1,0:T(8,128)(2,1)S(1)}, u32[]{:S(2)}, u32[]{:S(2)}) %collective-permute-start.31) | collective-permute-done | bytes 147488 | tf_op jit(solution)/shard_map/ppermute | solution.py:835
  222.8 1.1 maximum_convert_fusion.1
  223.9 5.2 %collective-permute-done.30.refs_1_ = bf16[784,384]{1,0:T(8,128)(2,1)S(1)} collective-permute-done((bf16[784,384]{1,0:T(8,128)(2,1)S(1)}, bf16[784,384]{1,0:T(8,128)(2,1)S(1)}, u32[]{:S(2)}, u32[]{:S(2)}) %collective-permute-start.30) | collective-permute-done | bytes 602144 | tf_op jit(solution)/shard_map/ppermute | solution.py:843
  229.7 2.2 collective-permute-start.35
  231.9 2.2 collective-permute-start.36
  235.3 1.4 collective-permute-done.34.refs_1_
  236.6 7.2 %collective-permute-done.35.refs_2_ = bf16[208,384]{1,0:T(8,128)(2,1)S(1)} collective-permute-done((bf16[208,384]{1,0:T(8,128)(2,1)S(1)}, bf16[208,384]{1,0:T(8,128)(2,1)S(1)}, u32[]{:S(2)}, u32[]{:S(2)}) %collective-permute-start.35) | collective-permute-done | bytes 159776 | tf_op jit(solution)/shard_map/ppermute | solution.py:839
  244.6 4.7 %collective-permute-done.37 = bf16[208,384]{1,0:T(8,128)(2,1)S(1)} collective-permute-done((bf16[208,384]{1,0:T(8,128)(2,1)S(1)}, bf16[208,384]{1,0:T(8,128)(2,1)S(1)}, u32[]{:S(2)}, u32[]{:S(2)}) %collective-permute-start.37) | collective-permute-done | bytes 159776 | tf_op jit(solution)/shard_map/ppermute | solution.py:835
  249.4 1.6 collective-permute-done.38.refs_2_
  251.0 1.6 finish.1
  (166 shorter events, 18.7 us)
Async XLA Ops:
  7.3 82.7 %all-gather.3.cloned.1.call-start = ((), (), s32[]{:S(2)}) async-start(), calls=%async_computation | async-start | bytes 4866048 | tf_op jit(solution)/shard_map/all_gather | solution.py:1172
  9.9 9.6 %collective-permute-start = (bf16[208,384]{1,0:T(8,128)(2,1)S(1)}, bf16[208,384]{1,0:T(8,128)(2,1)S(1)}, u32[]{:S(2)}, u32[]{:S(2)}) collective-permute-start(bf16[208,384]{1,0:T(8,128)(2,1)S(1)} %get-tuple-element.223), channel_id=1, source_target_pairs={{0,2},{1,3},{2,0},{3,1},{4,6},{5,7},{6,4},{7,5},{8,10},{9,11},{10,... | collective-permute-start | bytes 479240 | tf_op jit(solution)/shard_map/ppermute | solution.py:839
  13.0 15.8 %collective-permute-start.1 = (bf16[208,384]{1,0:T(8,128)(2,1)S(1)}, bf16[208,384]{1,0:T(8,128)(2,1)S(1)}, u32[]{:S(2)}, u32[]{:S(2)}) collective-permute-start(bf16[208,384]{1,0:T(8,128)(2,1)S(1)} %get-tuple-element.223), channel_id=1, source_target_pairs={{0,4},{1,5},{2,6},{3,7},{4,0},{5,1},{6,2},{7,3},{8,12},{9,13},{10,... | collective-permute-start | bytes 479240 | tf_op jit(solution)/shard_map/ppermute | solution.py:839
  15.5 13.3 %collective-permute-start.2 = (bf16[208,384]{1,0:T(8,128)(2,1)S(1)}, bf16[208,384]{1,0:T(8,128)(2,1)S(1)}, u32[]{:S(2)}, u32[]{:S(2)}) collective-permute-start(bf16[208,384]{1,0:T(8,128)(2,1)S(1)} %get-tuple-element.223), channel_id=1, source_target_pairs={{0,6},{1,7},{2,4},{3,5},{4,2},{5,3},{6,0},{7,1},{8,14},{9,15},{10,... | collective-permute-start | bytes 479240 | tf_op jit(solution)/shard_map/ppermute | solution.py:839
  28.9 13.8 %copy-start.5 = (f32[96,3072]{1,0:T(8,128)S(1)}, f32[96,3072]{1,0:T(8,128)}, u32[]{:S(2)}) copy-start(f32[96,3072]{1,0:T(8,128)} %param.29) | copy-start | bytes 3538948
  28.9 12.1 %collective-permute-start.3 = (bf16[4,208,384]{2,1,0:T(8,128)(2,1)S(1)}, bf16[4,208,384]{2,1,0:T(8,128)(2,1)S(1)}, u32[]{:S(2)}, u32[]{:S(2)}) collective-permute-start(bf16[4,208,384]{2,1,0:T(8,128)(2,1)S(1)} %pad_maximum_fusion), channel_id=1, source_target_pairs={{0,16},{1,17},{2,18},{3,19},{4,20},{5,21},{6,22},{7,23},{8,9},{9,8... | collective-permute-start | bytes 1916936 | tf_op jit(solution)/shard_map/ppermute | solution.py:843
  41.1 21.5 %copy-start.8 = (bf16[8,208,384]{2,1,0:T(8,128)(2,1)}, bf16[8,208,384]{2,1,0:T(8,128)(2,1)S(1)}, u32[]{:S(2)}) copy-start(bf16[8,208,384]{2,1,0:T(8,128)(2,1)S(1)} %constant_dynamic-update-slice_fusion.refs_5_) | copy-start | bytes 3833860
  41.1 21.2 %collective-permute-start.7 = (bf16[8,208,384]{2,1,0:T(8,128)(2,1)S(1)}, bf16[8,208,384]{2,1,0:T(8,128)(2,1)}, u32[]{:S(2)}, u32[]{:S(2)}) collective-permute-start(bf16[8,208,384]{2,1,0:T(8,128)(2,1)S(1)} %constant_dynamic-update-slice_fusion.refs_5_), channel_id=1, source_target_pairs={{0,1},{1,0},{2,3},{3,2},{4,5},{5,4},{6,7},{7,6},{8,24},{9,25},{10,... | collective-permute-start | bytes 3833864 | tf_op jit(solution)/shard_map/ppermute | solution.py:843
  42.7 19.7 %collective-permute-start.8 = (bf16[8,208,384]{2,1,0:T(8,128)(2,1)S(1)}, bf16[8,208,384]{2,1,0:T(8,128)(2,1)S(1)}, u32[]{:S(2)}, u32[]{:S(2)}) collective-permute-start(bf16[8,208,384]{2,1,0:T(8,128)(2,1)S(1)} %constant_dynamic-update-slice_fusion.refs_5_), channel_id=1, source_target_pairs={{0,8},{1,9},{2,10},{3,11},{4,12},{5,13},{6,14},{7,15},{8,0},{9,1},... | collective-permute-start | bytes 3833864 | tf_op jit(solution)/shard_map/ppermute | solution.py:831
  42.8 13.9 %collective-permute-start.4 = (bf16[48,1536]{1,0:T(8,128)(2,1)S(1)}, bf16[48,1536]{1,0:T(8,128)(2,1)S(1)}, u32[]{:S(2)}, u32[]{:S(2)}) collective-permute-start(bf16[48,1536]{1,0:T(8,128)(2,1)S(1)} %fusion.2), channel_id=1, source_target_pairs={{0,2},{1,3},{2,0},{3,1},{4,6},{5,7},{6,4},{7,5},{8,10},{9,11},{10,... | collective-permute-start | bytes 442376 | tf_op jit(solution)/shard_map/ppermute | solution.py:839
  45.3 11.9 %collective-permute-start.5 = (bf16[48,1536]{1,0:T(8,128)(2,1)S(1)}, bf16[48,1536]{1,0:T(8,128)(2,1)S(1)}, u32[]{:S(2)}, u32[]{:S(2)}) collective-permute-start(bf16[48,1536]{1,0:T(8,128)(2,1)S(1)} %fusion.2), channel_id=1, source_target_pairs={{0,4},{1,5},{2,6},{3,7},{4,0},{5,1},{6,2},{7,3},{8,12},{9,13},{10,... | collective-permute-start | bytes 442376 | tf_op jit(solution)/shard_map/ppermute | solution.py:839
  47.1 15.2 %collective-permute-start.6 = (bf16[48,1536]{1,0:T(8,128)(2,1)S(1)}, bf16[48,1536]{1,0:T(8,128)(2,1)S(1)}, u32[]{:S(2)}, u32[]{:S(2)}) collective-permute-start(bf16[48,1536]{1,0:T(8,128)(2,1)S(1)} %fusion.2), channel_id=1, source_target_pairs={{0,6},{1,7},{2,4},{3,5},{4,2},{5,3},{6,0},{7,1},{8,14},{9,15},{10,... | collective-permute-start | bytes 442376 | tf_op jit(solution)/shard_map/ppermute | solution.py:839
  62.2 5.2 %copy-start.3 = (s32[8]{0:T(128)S(1)}, s32[8]{0:T(128)}, u32[]{:S(2)}) copy-start(s32[8]{0:T(128)} %refs_1_.4) | copy-start | bytes 100
  62.3 5.2 %copy-start.4 = (s32[8]{0:T(128)S(1)}, s32[8]{0:T(128)}, u32[]{:S(2)}) copy-start(s32[8]{0:T(128)} %refs_2_.4) | copy-start | bytes 100
  62.4 3.4 %collective-permute-start.9 = (bf16[8,208,384]{2,1,0:T(8,128)(2,1)}, bf16[8,208,384]{2,1,0:T(8,128)(2,1)}, u32[]{:S(2)}, u32[]{:S(2)}) collective-permute-start(bf16[8,208,384]{2,1,0:T(8,128)(2,1)} %collective-permute-done.7.refs_6_), channel_id=1, source_target_pairs={{0,8},{1,9},{2,10},{3,11},{4,12},{5,13},{6,14},{7,15},{8,0},{9,1},... | collective-permute-start | bytes 3833864 | tf_op jit(solution)/shard_map/ppermute | solution.py:831
  63.5 22.5 %collective-permute-start.10 = (bf16[4,48,1536]{2,1,0:T(8,128)(2,1)S(1)}, bf16[4,48,1536]{2,1,0:T(8,128)(2,1)S(1)}, u32[]{:S(2)}, u32[]{:S(2)}) collective-permute-start(bf16[4,48,1536]{2,1,0:T(8,128)(2,1)S(1)} %pad_maximum_fusion.1.refs_9_), channel_id=1, source_target_pairs={{0,16},{1,17},{2,18},{3,19},{4,20},{5,21},{6,22},{7,23},{8,9},{9,8... | collective-permute-start | bytes 1769480 | tf_op jit(solution)/shard_map/ppermute | solution.py:843
  86.0 16.4 %copy-start = (bf16[8,48,1536]{2,1,0:T(8,128)(2,1)}, bf16[8,48,1536]{2,1,0:T(8,128)(2,1)S(1)}, u32[]{:S(2)}) copy-start(bf16[8,48,1536]{2,1,0:T(8,128)(2,1)S(1)} %constant_dynamic-update-slice_fusion.5.refs_4_.refs_8_) | copy-start | bytes 3538948
  86.0 16.7 %collective-permute-start.11 = (bf16[8,48,1536]{2,1,0:T(8,128)(2,1)S(1)}, bf16[8,48,1536]{2,1,0:T(8,128)(2,1)}, u32[]{:S(2)}, u32[]{:S(2)}) collective-permute-start(bf16[8,48,1536]{2,1,0:T(8,128)(2,1)S(1)} %constant_dynamic-update-slice_fusion.5.refs_4_.refs_8_), channel_id=1, source_target_pairs={{0,1},{1,0},{2,3},{3,2},{4,5},{5,4},{6,7},{7,6},{8,24},{9,25},{10,... | collective-permute-start | bytes 3538952 | tf_op jit(solution)/shard_map/ppermute | solution.py:843
  102.4 2.9 %collective-permute-start.12 = (bf16[8,48,1536]{2,1,0:T(8,128)(2,1)S(1)}, bf16[8,48,1536]{2,1,0:T(8,128)(2,1)S(1)}, u32[]{:S(2)}, u32[]{:S(2)}) collective-permute-start(bf16[8,48,1536]{2,1,0:T(8,128)(2,1)S(1)} %constant_dynamic-update-slice_fusion.5.refs_4_.refs_8_), channel_id=1, source_target_pairs={{0,8},{1,9},{2,10},{3,11},{4,12},{5,13},{6,14},{7,15},{8,0},{9,1},... | collective-permute-start | bytes 3538952 | tf_op jit(solution)/shard_map/ppermute | solution.py:831
  102.8 4.5 %collective-permute-start.13 = (bf16[8,48,1536]{2,1,0:T(8,128)(2,1)}, bf16[8,48,1536]{2,1,0:T(8,128)(2,1)S(1)}, u32[]{:S(2)}, u32[]{:S(2)}) collective-permute-start(bf16[8,48,1536]{2,1,0:T(8,128)(2,1)} %collective-permute-done.11.refs_9_), channel_id=1, source_target_pairs={{0,8},{1,9},{2,10},{3,11},{4,12},{5,13},{6,14},{7,15},{8,0},{9,1},... | collective-permute-start | bytes 3538952 | tf_op jit(solution)/shard_map/ppermute | solution.py:831
  127.8 5.7 %collective-permute-start.14 = (bf16[16,192,384]{2,1,0:T(8,128)(2,1)}, bf16[16,192,384]{2,1,0:T(8,128)(2,1)S(1)}, u32[]{:S(2)}, u32[]{:S(2)}) collective-permute-start(bf16[16,192,384]{2,1,0:T(8,128)(2,1)} %get-tuple-element.133), channel_id=1, source_target_pairs={{0,8},{1,9},{2,10},{3,11},{4,12},{5,13},{6,14},{7,15},{8,0},{9,1},... | collective-permute-start | bytes 7077896 | tf_op jit(solution)/shard_map/ppermute | solution.py:831
  134.0 16.5 %collective-permute-start.15 = (bf16[1536,384]{1,0:T(8,128)(2,1)S(1)}, bf16[1536,384]{1,0:T(8,128)(2,1)S(1)}, u32[]{:S(2)}, u32[]{:S(2)}) collective-permute-start(bf16[1536,384]{1,0:T(8,128)(2,1)S(1)} %get-tuple-element.143), channel_id=1, source_target_pairs={{0,1},{1,0},{2,3},{3,2},{4,5},{5,4},{6,7},{7,6},{8,24},{9,25},{10,... | collective-permute-start | bytes 3538952 | tf_op jit(solution)/shard_map/ppermute | solution.py:843
  150.9 10.6 %collective-permute-start.17 = (bf16[16,192,384]{2,1,0:T(8,128)(2,1)S(1)}, bf16[16,192,384]{2,1,0:T(8,128)(2,1)S(1)}, u32[]{:S(2)}, u32[]{:S(2)}) collective-permute-start(bf16[16,192,384]{2,1,0:T(8,128)(2,1)S(1)} %copy-done.19), channel_id=1, source_target_pairs={{0,8},{1,9},{2,10},{3,11},{4,12},{5,13},{6,14},{7,15},{8,0},{9,1},... | collective-permute-start | bytes 7077896 | tf_op jit(solution)/shard_map/ppermute | solution.py:831
  150.9 11.8 %collective-permute-start.16 = (bf16[768,384]{1,0:T(8,128)(2,1)S(1)}, bf16[768,384]{1,0:T(8,128)(2,1)S(1)}, u32[]{:S(2)}, u32[]{:S(2)}) collective-permute-start(bf16[768,384]{1,0:T(8,128)(2,1)S(1)} %get-tuple-element.153), channel_id=1, source_target_pairs={{0,16},{1,17},{2,18},{3,19},{4,20},{5,21},{6,22},{7,23},{8,9},{9,8... | collective-permute-start | bytes 1769480 | tf_op jit(solution)/shard_map/ppermute | solution.py:843
  162.0 19.9 %collective-permute-start.18 = (bf16[1536,384]{1,0:T(8,128)(2,1)S(1)}, bf16[1536,384]{1,0:T(8,128)(2,1)S(1)}, u32[]{:S(2)}, u32[]{:S(2)}) collective-permute-start(bf16[1536,384]{1,0:T(8,128)(2,1)S(1)} %get-tuple-element.167), channel_id=1, source_target_pairs={{0,1},{1,0},{2,3},{3,2},{4,5},{5,4},{6,7},{7,6},{8,24},{9,25},{10,... | collective-permute-start | bytes 3538952 | tf_op jit(solution)/shard_map/ppermute | solution.py:843
  162.9 21.4 %collective-permute-start.19 = (bf16[192,384]{1,0:T(8,128)(2,1)S(1)}, bf16[192,384]{1,0:T(8,128)(2,1)S(1)}, u32[]{:S(2)}, u32[]{:S(2)}) collective-permute-start(bf16[192,384]{1,0:T(8,128)(2,1)S(1)} %get-tuple-element.172), channel_id=1, source_target_pairs={{0,2},{1,3},{2,0},{3,1},{4,6},{5,7},{6,4},{7,5},{8,10},{9,11},{10,... | collective-permute-start | bytes 442376 | tf_op jit(solution)/shard_map/ppermute | solution.py:839
  164.8 19.5 %collective-permute-start.20 = (bf16[192,384]{1,0:T(8,128)(2,1)S(1)}, bf16[192,384]{1,0:T(8,128)(2,1)S(1)}, u32[]{:S(2)}, u32[]{:S(2)}) collective-permute-start(bf16[192,384]{1,0:T(8,128)(2,1)S(1)} %get-tuple-element.173), channel_id=1, source_target_pairs={{0,4},{1,5},{2,6},{3,7},{4,0},{5,1},{6,2},{7,3},{8,12},{9,13},{10,... | collective-permute-start | bytes 442376 | tf_op jit(solution)/shard_map/ppermute | solution.py:839
  165.4 18.8 %collective-permute-start.21 = (bf16[192,384]{1,0:T(8,128)(2,1)S(1)}, bf16[192,384]{1,0:T(8,128)(2,1)S(1)}, u32[]{:S(2)}, u32[]{:S(2)}) collective-permute-start(bf16[192,384]{1,0:T(8,128)(2,1)S(1)} %get-tuple-element.174), channel_id=1, source_target_pairs={{0,6},{1,7},{2,4},{3,5},{4,2},{5,3},{6,0},{7,1},{8,14},{9,15},{10,... | collective-permute-start | bytes 442376 | tf_op jit(solution)/shard_map/ppermute | solution.py:839
  167.3 13.7 %copy-start.1 = (f32[3,32,16]{2,1,0:T(8,128)S(1)}, f32[3,32,16]{2,1,0:T(8,128)}, u32[]{:S(2)}) copy-start(f32[3,32,16]{2,1,0:T(8,128)} %constant.117.clone.refs_1_) | copy-start | bytes 18436
  167.3 13.7 %copy-start.2 = (f32[3,32,8]{2,1,0:T(8,128)S(1)}, f32[3,32,8]{2,1,0:T(8,128)}, u32[]{:S(2)}) copy-start(f32[3,32,8]{2,1,0:T(8,128)} %constant.118.clone.refs_2_) | copy-start | bytes 9220
  181.8 10.3 %collective-permute-start.22 = (bf16[16,384]{1,0:T(8,128)(2,1)S(1)}, bf16[16,384]{1,0:T(8,128)(2,1)S(1)}, u32[]{:S(2)}, u32[]{:S(2)}) collective-permute-start(bf16[16,384]{1,0:T(8,128)(2,1)S(1)} %get-tuple-element.171.refs_6_), channel_id=1, source_target_pairs={{0,8},{1,9},{2,10},{3,11},{4,12},{5,13},{6,14},{7,15},{8,0},{9,1},... | collective-permute-start | bytes 36872 | tf_op jit(solution)/shard_map/ppermute | solution.py:831
  182.2 9.9 %collective-permute-start.23 = (bf16[768,384]{1,0:T(8,128)(2,1)S(1)}, bf16[768,384]{1,0:T(8,128)(2,1)S(1)}, u32[]{:S(2)}, u32[]{:S(2)}) collective-permute-start(bf16[768,384]{1,0:T(8,128)(2,1)S(1)} %get-tuple-element.177), channel_id=1, source_target_pairs={{0,16},{1,17},{2,18},{3,19},{4,20},{5,21},{6,22},{7,23},{8,9},{9,8... | collective-permute-start | bytes 1769480 | tf_op jit(solution)/shard_map/ppermute | solution.py:843
  184.3 8.1 %copy-start.11 = (pred[16]{0:T(512)(128)(4,1)S(1)}, pred[16]{0:T(512)(128)(4,1)}, u32[]{:S(2)}) copy-start(pred[16]{0:T(512)(128)(4,1)} %constant.116.clone.1) | copy-start | bytes 52
  192.2 4.8 %collective-permute-start.24 = (bf16[16,192,384]{2,1,0:T(8,128)(2,1)}, bf16[16,192,384]{2,1,0:T(8,128)(2,1)S(1)}, u32[]{:S(2)}, u32[]{:S(2)}) collective-permute-start(bf16[16,192,384]{2,1,0:T(8,128)(2,1)} %get-tuple-element.180), channel_id=1, source_target_pairs={{0,8},{1,9},{2,10},{3,11},{4,12},{5,13},{6,14},{7,15},{8,0},{9,1},... | collective-permute-start | bytes 7077896 | tf_op jit(solution)/shard_map/ppermute | solution.py:831
  192.5 21.0 %collective-permute-start.27 = (bf16[192,384]{1,0:T(8,128)(2,1)S(1)}, bf16[192,384]{1,0:T(8,128)(2,1)S(1)}, u32[]{:S(2)}, u32[]{:S(2)}) collective-permute-start(bf16[192,384]{1,0:T(8,128)(2,1)S(1)} %get-tuple-element.190), channel_id=1, source_target_pairs={{0,2},{1,3},{2,0},{3,1},{4,6},{5,7},{6,4},{7,5},{8,10},{9,11},{10,... | collective-permute-start | bytes 442376 | tf_op jit(solution)/shard_map/ppermute | solution.py:839
  193.4 20.2 %collective-permute-start.28 = (bf16[192,384]{1,0:T(8,128)(2,1)S(1)}, bf16[192,384]{1,0:T(8,128)(2,1)S(1)}, u32[]{:S(2)}, u32[]{:S(2)}) collective-permute-start(bf16[192,384]{1,0:T(8,128)(2,1)S(1)} %get-tuple-element.191), channel_id=1, source_target_pairs={{0,4},{1,5},{2,6},{3,7},{4,0},{5,1},{6,2},{7,3},{8,12},{9,13},{10,... | collective-permute-start | bytes 442376 | tf_op jit(solution)/shard_map/ppermute | solution.py:839
  194.9 18.6 %collective-permute-start.29 = (bf16[192,384]{1,0:T(8,128)(2,1)S(1)}, bf16[192,384]{1,0:T(8,128)(2,1)S(1)}, u32[]{:S(2)}, u32[]{:S(2)}) collective-permute-start(bf16[192,384]{1,0:T(8,128)(2,1)S(1)} %get-tuple-element.192), channel_id=1, source_target_pairs={{0,6},{1,7},{2,4},{3,5},{4,2},{5,3},{6,0},{7,1},{8,14},{9,15},{10,... | collective-permute-start | bytes 442376 | tf_op jit(solution)/shard_map/ppermute | solution.py:839
  197.6 6.7 %collective-permute-start.26 = (bf16[192,384]{1,0:T(8,128)(2,1)S(1)}, bf16[192,384]{1,0:T(8,128)(2,1)S(1)}, u32[]{:S(2)}, u32[]{:S(2)}) collective-permute-start(bf16[192,384]{1,0:T(8,128)(2,1)S(1)} %total.3.refs_4_), channel_id=1, source_target_pairs={{0,16},{1,17},{2,18},{3,19},{4,20},{5,21},{6,22},{7,23},{8,24},{9,... | collective-permute-start | bytes 442376 | tf_op jit(solution)/shard_map/ppermute | solution.py:835
  199.6 16.3 %collective-permute-start.25 = (bf16[1552,384]{1,0:T(8,128)(2,1)S(1)}, bf16[1552,384]{1,0:T(8,128)(2,1)S(1)}, u32[]{:S(2)}, u32[]{:S(2)}) collective-permute-start(bf16[1552,384]{1,0:T(8,128)(2,1)S(1)} %get-tuple-element.188), channel_id=1, source_target_pairs={{0,1},{1,0},{2,3},{3,2},{4,5},{5,4},{6,7},{7,6},{8,24},{9,25},{10,... | collective-permute-start | bytes 3575816 | tf_op jit(solution)/shard_map/ppermute | solution.py:843
  204.5 12.1 %collective-permute-start.33 = (bf16[48,3072]{1,0:T(8,128)(2,1)S(1)}, bf16[48,3072]{1,0:T(8,128)(2,1)S(1)}, u32[]{:S(2)}, u32[]{:S(2)}) collective-permute-start(bf16[48,3072]{1,0:T(8,128)(2,1)S(1)} %pad_maximum_fusion.4), channel_id=1, source_target_pairs={{0,8},{1,9},{2,10},{3,11},{4,12},{5,13},{6,14},{7,15},{8,0},{9,1},... | collective-permute-start | bytes 884744 | tf_op jit(solution)/shard_map/ppermute | solution.py:831
  216.4 6.2 %collective-permute-start.31 = (bf16[192,384]{1,0:T(8,128)(2,1)S(1)}, bf16[192,384]{1,0:T(8,128)(2,1)S(1)}, u32[]{:S(2)}, u32[]{:S(2)}) collective-permute-start(bf16[192,384]{1,0:T(8,128)(2,1)S(1)} %total.4), channel_id=1, source_target_pairs={{0,16},{1,17},{2,18},{3,19},{4,20},{5,21},{6,22},{7,23},{8,24},{9,... | collective-permute-start | bytes 442376 | tf_op jit(solution)/shard_map/ppermute | solution.py:835
  216.6 12.4 %collective-permute-start.30 = (bf16[784,384]{1,0:T(8,128)(2,1)S(1)}, bf16[784,384]{1,0:T(8,128)(2,1)S(1)}, u32[]{:S(2)}, u32[]{:S(2)}) collective-permute-start(bf16[784,384]{1,0:T(8,128)(2,1)S(1)} %get-tuple-element.194), channel_id=1, source_target_pairs={{0,16},{1,17},{2,18},{3,19},{4,20},{5,21},{6,22},{7,23},{8,9},{9,8... | collective-permute-start | bytes 1806344 | tf_op jit(solution)/shard_map/ppermute | solution.py:843
  222.7 11.4 %collective-permute-start.32 = (bf16[192,768]{1,0:T(8,128)(2,1)S(1)}, bf16[192,768]{1,0:T(8,128)(2,1)S(1)}, u32[]{:S(2)}, u32[]{:S(2)}) collective-permute-start(bf16[192,768]{1,0:T(8,128)(2,1)S(1)} %pad_maximum_fusion.3), channel_id=1, source_target_pairs={{0,8},{1,9},{2,10},{3,11},{4,12},{5,13},{6,14},{7,15},{8,0},{9,1},... | collective-permute-start | bytes 884744 | tf_op jit(solution)/shard_map/ppermute | solution.py:831
  229.7 6.9 %collective-permute-start.34 = (bf16[208,384]{1,0:T(8,128)(2,1)S(1)}, bf16[208,384]{1,0:T(8,128)(2,1)S(1)}, u32[]{:S(2)}, u32[]{:S(2)}) collective-permute-start(bf16[208,384]{1,0:T(8,128)(2,1)S(1)} %get-tuple-element.199), channel_id=1, source_target_pairs={{0,2},{1,3},{2,0},{3,1},{4,6},{5,7},{6,4},{7,5},{8,10},{9,11},{10,... | collective-permute-start | bytes 479240 | tf_op jit(solution)/shard_map/ppermute | solution.py:839
  229.7 14.1 %collective-permute-start.35 = (bf16[208,384]{1,0:T(8,128)(2,1)S(1)}, bf16[208,384]{1,0:T(8,128)(2,1)S(1)}, u32[]{:S(2)}, u32[]{:S(2)}) collective-permute-start(bf16[208,384]{1,0:T(8,128)(2,1)S(1)} %get-tuple-element.200), channel_id=1, source_target_pairs={{0,4},{1,5},{2,6},{3,7},{4,0},{5,1},{6,2},{7,3},{8,12},{9,13},{10,... | collective-permute-start | bytes 479240 | tf_op jit(solution)/shard_map/ppermute | solution.py:839
  231.9 11.9 %collective-permute-start.36 = (bf16[208,384]{1,0:T(8,128)(2,1)S(1)}, bf16[208,384]{1,0:T(8,128)(2,1)S(1)}, u32[]{:S(2)}, u32[]{:S(2)}) collective-permute-start(bf16[208,384]{1,0:T(8,128)(2,1)S(1)} %get-tuple-element.201), channel_id=1, source_target_pairs={{0,6},{1,7},{2,4},{3,5},{4,2},{5,3},{6,0},{7,1},{8,14},{9,15},{10,... | collective-permute-start | bytes 479240 | tf_op jit(solution)/shard_map/ppermute | solution.py:839
  243.9 5.3 %collective-permute-start.37 = (bf16[208,384]{1,0:T(8,128)(2,1)S(1)}, bf16[208,384]{1,0:T(8,128)(2,1)S(1)}, u32[]{:S(2)}, u32[]{:S(2)}) collective-permute-start(bf16[208,384]{1,0:T(8,128)(2,1)S(1)} %total.5), channel_id=1, source_target_pairs={{0,16},{1,17},{2,18},{3,19},{4,20},{5,21},{6,22},{7,23},{8,24},{9,... | collective-permute-start | bytes 479240 | tf_op jit(solution)/shard_map/ppermute | solution.py:835
  249.3 1.7 collective-permute-start.38
  (13 other events, 31.0 us)
Sparse Core Ops, SparseCore 0:
  11.6 78.3 all-gather.2
